TPU v7x, 32 devices: a whole 2x2x4 slice. The times are simulated.
32 devices in a mesh: blk: 4 (over x, core), grp: 8 (over z, y).
Axes of the slice: x: 2, y: 2, z: 4, core: 2. Of those that a mesh axis runs over, the one named last changes fastest.
Arguments:
- amplitudes: bfloat16 [1536, 1024], P(('blk', 'grp')), may hold values from -6 to 6
- integrals: bfloat16 [1024, 8192], P(None, ('grp', 'blk')), may hold values from -0.1875 to 0.1875
- amplitude_mask: int32 [96, 8], P(('blk', 'grp')), may hold values 0 or 1
- integral_mask: int32 [8, 64], P(None, ('grp', 'blk')), may hold values 0 or 1
Outputs:
- residual: bfloat16 [1536, 8192], P('blk', 'grp')
All inputs are finite; a program needn't handle non-finite values. No bound on the sum of `amplitude_mask` or of `integral_mask` on one device may be relied on, other than what follows from the above.
Results may differ from a plain program's by a relative error of at most 0.001.
Values may be sent and summed in bfloat16 or wider, within the bound.
No kernel may reach another device: no remote copies, remote signals or barrier semaphores. Data moves between devices by JAX's collectives and lax.ppermute only.
A program may use at most 64 MiB of HBM per device.

v0:
```python
import jax
import jax.numpy as jnp
from jax import lax
from jax.sharding import PartitionSpec as P

TILE = 128
OTILE = 16


def mask_tiles(values, screen, row_tile, col_tile):
    height, breadth = values.shape
    tiled = values.reshape(height // row_tile, row_tile, breadth // col_tile, col_tile)
    tiled = tiled * screen.astype(values.dtype)[:, None, :, None]
    return tiled.reshape(height, breadth)


def local(amplitudes, integrals, amplitude_mask, integral_mask):
    amp_masked = mask_tiles(amplitudes, amplitude_mask, OTILE, TILE)
    int_panel = mask_tiles(integrals, integral_mask, TILE, TILE)
    gathered = lax.all_gather(amp_masked, "grp", axis=0, tiled=True)
    return (
        0.5
        * jnp.dot(
            gathered,
            lax.all_gather(int_panel, "blk", axis=1, tiled=True),
            preferred_element_type=jnp.float32,
        )
    ).astype(jnp.bfloat16)


def solution(mesh):
    return jax.shard_map(
        local,
        mesh=mesh,
        in_specs=(
            P(("blk", "grp"), None),
            P(None, ("grp", "blk")),
            P(("blk", "grp"), None),
            P(None, ("grp", "blk")),
        ),
        out_specs=P("blk", "grp"),
        check_vma=False,
    )
```

profile of v0, /device:TPU:0, one launch (start us, length us, event | category | flops | bytes accessed | tf_op | source)
XLA Modules:
  0.0 54.0 jit_solution(4516927587839036713)
XLA Ops:
  6.5 0.0 copy-start.1
  6.5 0.0 copy-start
  6.5 0.0 all-gather.2.cloned.1.call-start
  6.5 0.7 %convert_element_type.10 = bf16[8,2]{0,1:T(2,128)(2,1)S(1)} convert(s32[8,2]{0,1:T(2,128)} %param.7) | non-fusion elementwise | flops 16 | bytes 96 | tf_op jit(solution)/shard_map/convert_element_type | solution.py:13
  7.3 0.1 copy.5
  7.4 0.3 mul.31
  7.7 1.9 %bitcast_multiply_fusion = bf16[1024,256]{1,0:T(8,128)(2,1)} fusion(bf16[1024,256]{1,0:T(8,128)(2,1)} %param.5, bf16[128,8,2,128]{3,2,1,0:T(2,128)(2,1)S(1)} %bitcast.10), kind=kLoop, calls=%fused_computation.1 | loop fusion | flops 262144 | bytes 1572864 | tf_op jit(solution)/shard_map/mul | solution.py:13
  9.6 0.0 all-gather.2.cloned.1.call-update
  9.6 0.0 copy-done.1
  9.7 0.1 mul.28
  9.8 0.0 copy-done
  9.8 33.8 %all_gather.6 = bf16[384,1024]{1,0:T(8,128)(2,1)S(1)} all-gather(bf16[48,1024]{1,0:T(8,128)(2,1)S(1)} %bitcast_multiply_fusion.1), channel_id=1, replica_groups=mesh['blk'=4,'grp'=8] {'grp'}, dimensions={0}, use_global_device_ids=true | all-gather | bytes 884736 | tf_op jit(solution)/shard_map/all_gather | solution.py:20
  43.6 0.0 all-gather.2.cloned.1.call-done
  43.6 3.5 %multiply_convert_fusion = bf16[384,1024]{1,0:T(8,128)(2,1)} fusion(bf16[384,1024]{1,0:T(8,128)(2,1)S(1)} %all_gather.6, bf16[1024,1024]{1,0:T(8,128)(2,1)} %all-gather.2.cloned.1.call-done), kind=kOutput, calls=%fused_computation | convolution fusion | flops 806092800 | bytes 3670016 | tf_op jit(solution)/shard_map/dot_general | solution.py:23
  (2 shorter events, 0.0 us)
Async XLA Ops:
  6.5 3.1 %copy-start.1 = (s32[3,8]{1,0:T(4,128)S(1)}, s32[3,8]{1,0:T(4,128)}, u32[]{:S(2)}) copy-start(s32[3,8]{1,0:T(4,128)} %param.6) | copy-start | bytes 292
  6.5 3.2 %copy-start = (bf16[48,1024]{1,0:T(8,128)(2,1)S(1)}, bf16[48,1024]{1,0:T(8,128)(2,1)}, u32[]{:S(2)}) copy-start(bf16[48,1024]{1,0:T(8,128)(2,1)} %param.4) | copy-start | bytes 294916
  6.5 37.1 %all-gather.2.cloned.1.call-start = ((), (), s32[]{:S(2)}) async-start(), calls=%async_computation | async-start | bytes 2621440 | tf_op jit(solution)/shard_map/all_gather | solution.py:25
Sparse Core Ops, SparseCore 0:
  9.8 25.5 all-gather.1
where the time goes:
time: 54.2 us; the launch traced here: 54 us
  blocking collectives  33.8 us (62%)
  between operations  13.4 us (25%)
  matrix products  3.47 us (6%)
  other arithmetic  2.66 us (5%)
    all_gather x1, blocking collectives, local(): gathered = lax.all_gather(amp_masked, 'grp', axis=0, tiled=True)  33.8 us
    dot_general x1, matrix products, local(): jnp.dot(gathered, lax.all_gather(int_panel, 'blk', axis=1, tiled=True), p...  3.47 us
    mul x2, other arithmetic, mask_tiles(): tiled = tiled * screen.astype(values.dtype)[:, None, :, None]  1.94 us
  transfers between devices with their start and end apart: 1, of which 0 were waited for; matrix products, arithmetic and copies ran while one was open for 0% of the time, Pallas kernels for 0%

commit v1 on v0

v1 whole, which is shorter than its diff:
```python
import functools
import jax
import jax.numpy as jnp
from jax import lax
from jax.experimental import pallas as pl
from jax.experimental.pallas import tpu as pltpu
from jax.sharding import PartitionSpec as P

TILE = 128
OTILE = 16
VMEM = pl.BlockSpec(memory_space=pltpu.VMEM)
SMEM = pl.BlockSpec(memory_space=pltpu.SMEM)


def limit(*values):
    nbytes = sum(v.size * v.dtype.itemsize for v in values)
    return pltpu.CompilerParams(vmem_limit_bytes=2 * nbytes + 4 * 2**20)


def after(v, *deps):
    return lax.optimization_barrier((v, *deps))[0]


def held(v):
    return pltpu.with_memory_space_constraint(v, pltpu.VMEM)


def mask_kernel(amask, bmask, a, b, a_out, b_out):
    def factor(mask, i, j):
        return mask[i, j].astype(jnp.float32).astype(a.dtype)

    for i in range(a.shape[0] // OTILE):
        for j in range(a.shape[1] // TILE):
            at = (slice(i * OTILE, (i + 1) * OTILE), slice(j * TILE, (j + 1) * TILE))
            a_out[at] = a[at] * factor(amask, i, j)
    for i in range(b.shape[0] // TILE):
        for j in range(b.shape[1] // TILE):
            at = (slice(i * TILE, (i + 1) * TILE), slice(j * TILE, (j + 1) * TILE))
            b_out[at] = b[at] * factor(bmask, j, i)


def product_kernel(n_grp, n_blk, *refs):
    a_refs, b_refs, (out, a_all, o_all, sems) = refs[:n_grp], refs[n_grp:-4], refs[-4:]
    g, q = lax.axis_index("grp"), lax.axis_index("blk")
    rows = a_refs[0].shape[0]
    for k, ref in enumerate(a_refs):
        a_all[pl.ds(pl.multiple_of((g ^ k) * rows, OTILE), rows), :] = ref[...]
    width = b_refs[0].shape[1]
    copies = []
    for k in range(n_blk):
        acc = jnp.dot(a_all[...], b_refs[k][...], preferred_element_type=jnp.float32)
        o_all[k] = (0.5 * acc).astype(out.dtype)
        cols = pl.ds(pl.multiple_of((q ^ k) * width, TILE), width)
        copies.append(pltpu.make_async_copy(o_all.at[k], out.at[:, cols], sems.at[k]))
        copies[-1].start()
    for c in copies:
        c.wait()


def local(n_blk, n_grp, a, b, amask, bmask):
    a_own, b_own = pl.pallas_call(
        mask_kernel,
        out_shape=[pltpu.VMEM(a.shape, a.dtype), pltpu.VMEM(b.shape, b.dtype)],
        in_specs=[SMEM, SMEM, VMEM, VMEM],
        out_specs=[VMEM, VMEM],
        compiler_params=limit(a, b),
    )(amask, bmask.T, a, b)

    def swap(v, axis, n, k):
        return lax.ppermute(v, axis, [(i, i ^ k) for i in range(n)])

    far = {k: swap(b_own, "blk", n_blk, k) for k in range(2, n_blk, 2)}
    direct = [1 << i for i in reversed(range(n_grp.bit_length() - 1))]
    got = lax.optimization_barrier([swap(a_own, "grp", n_grp, k) for k in direct])
    a_all = {0: a_own, **dict(zip(direct, got, strict=True))}
    for top in reversed(direct):
        for k in (*range(top // 2, top), *range(1, top // 2)):
            if k:
                a_all[top ^ k] = swap(a_all[top], "grp", n_grp, k)
    b_all = {0: b_own, 1: swap(after(b_own, a_all[n_grp * 3 // 4]), "blk", n_blk, 1)}
    for k, v in far.items():
        b_all |= {k: v, k ^ 1: swap(after(v, *a_all.values()), "blk", n_blk, 1)}
    a_all, b_all = ([d[k] for k in sorted(d)] for d in (a_all, b_all))
    rows, cols = a.shape[0] * n_grp, b.shape[1] * n_blk
    ops = [held(v) for v in a_all + b_all]
    out = jax.ShapeDtypeStruct((rows, cols), a.dtype)
    return pl.pallas_call(
        functools.partial(product_kernel, n_grp, n_blk),
        out_shape=out,
        in_specs=[VMEM] * len(ops),
        out_specs=pl.BlockSpec(memory_space=pl.ANY),
        scratch_shapes=[
            pltpu.VMEM((rows, a.shape[1]), a.dtype),
            pltpu.VMEM((n_blk, rows, b.shape[1]), a.dtype),
            pltpu.SemaphoreType.DMA((n_blk,)),
        ],
        compiler_params=limit(out, *a_all),
    )(*ops)


def solution(mesh):
    return jax.shard_map(
        functools.partial(local, mesh.shape["blk"], mesh.shape["grp"]),
        mesh=mesh,
        in_specs=(
            P(("blk", "grp"), None),
            P(None, ("grp", "blk")),
            P(("blk", "grp"), None),
            P(None, ("grp", "blk")),
        ),
        out_specs=P("blk", "grp"),
        check_vma=False,
    )
```

time: 54.2 us -> 28.9 us (0.53)
  blocking collectives: 33.8 us -> 0 us
  between operations: 13.4 us -> 0.03 us
  starting transfers between devices: 0.01 us -> 12.7 us
  waiting for transfers between devices: 0.02 us -> 10.1 us
  matrix products: 3.47 us -> 0 us
  local copies, waits for them, and re-layouts: 0.53 us -> 3.29 us
  other arithmetic: 2.66 us -> 0 us
  Pallas kernels: 0 us -> 2.55 us
    all_gather x1 -> x0, blocking collectives: 33.8 us -> none  [local(): gathered = lax.all_gather(amp_masked, 'grp', axis=0, tiled=True)]
    ppermute x0 -> x10, starting transfers between devices: none -> 12.7 us  [swap(): return lax.ppermute(v, axis, [(i, i ^ k) for i in range(n)])]
    ppermute x0 -> x10, waiting for transfers between devices: none -> 10.1 us  [swap(): return lax.ppermute(v, axis, [(i, i ^ k) for i in range(n)])]
    dot_general x1 -> x0, matrix products: 3.47 us -> none  [local(): jnp.dot(gathered, lax.all_gather(int_panel, 'blk', axis=1, tiled=True), p...]
    unnamed x4 -> x8, local copies, waits for them, and re-layouts: 0.01 us -> 3.29 us
    pallas_call x0 -> x2, Pallas kernels: none -> 2.55 us  [the longest x1 1.79 us: local(): pl.pallas_call(functools.partial(product_kernel, n_grp, n_blk), out_shape...]
    mul x2 -> x0, other arithmetic: 1.94 us -> none  [mask_tiles(): tiled = tiled * screen.astype(values.dtype)[:, None, :, None]]
    convert_element_type x2 -> x0, other arithmetic: 0.72 us -> none  [mask_tiles(): tiled = tiled * screen.astype(values.dtype)[:, None, :, None]]
  transfers between devices with their start and end apart: 1 -> 10, of which waited for: 0 -> 7; matrix products, arithmetic and copies ran while one was open for 0% -> 0% of each run, Pallas kernels for 0% -> 0%
where the time goes in v1:
time: 28.9 us; the launch traced here: 28.7 us
  starting transfers between devices  12.7 us (44%)
  waiting for transfers between devices  10.1 us (35%)
  local copies, waits for them, and re-layouts  3.29 us (11%)
  Pallas kernels  2.55 us (9%)
    ppermute x10, starting transfers between devices, swap(): return lax.ppermute(v, axis, [(i, i ^ k) for i in range(n)])  12.7 us
    ppermute x10, waiting for transfers between devices, swap(): return lax.ppermute(v, axis, [(i, i ^ k) for i in range(n)])  10.1 us
    unnamed x8, local copies, waits for them, and re-layouts  3.29 us
    pallas_call x1, Pallas kernels, local(): pl.pallas_call(functools.partial(product_kernel, n_grp, n_blk), out_shape...  1.79 us
    pallas_call x1, Pallas kernels, local(): pl.pallas_call(mask_kernel, out_shape=[pltpu.VMEM(a.shape, a.dtype), pltp...  0.75 us
  transfers between devices with their start and end apart: 10, of which 7 were waited for; matrix products, arithmetic and copies ran while one was open for 0% of the time, Pallas kernels for 0%

profile of v1, /device:TPU:0, one launch (start us, length us, event | category | flops | bytes accessed | tf_op | source)
XLA Modules:
  0.0 28.7 jit_solution(14930365667444842506)
XLA Ops:
  0.0 0.0 copy-start.3
  0.0 0.7 %copy-done.3 = s32[8,2]{0,1:T(2,128)S(1)} copy-done((s32[8,2]{0,1:T(2,128)S(1)}, s32[8,2]{0,1:T(2,128)}, u32[]{:S(2)}) %copy-start.3) | copy-done | bytes 88
  0.7 0.0 copy-start
  0.7 1.0 %copy-done = bf16[1024,256]{1,0:T(8,128)(2,1)S(1)} copy-done((bf16[1024,256]{1,0:T(8,128)(2,1)S(1)}, bf16[1024,256]{1,0:T(8,128)(2,1)}, u32[]{:S(2)}) %copy-start) | copy-done | bytes 524312
  1.7 0.0 copy-start.1
  1.7 0.9 %copy-done.1 = bf16[48,1024]{1,0:T(8,128)(2,1)S(1)} copy-done((bf16[48,1024]{1,0:T(8,128)(2,1)S(1)}, bf16[48,1024]{1,0:T(8,128)(2,1)}, u32[]{:S(2)}) %copy-start.1) | copy-done | bytes 98328
  2.6 0.0 copy-start.2
  2.6 0.7 %copy-done.2 = s32[3,8]{1,0:T(4,128)S(1)} copy-done((s32[3,8]{1,0:T(4,128)S(1)}, s32[3,8]{1,0:T(4,128)}, u32[]{:S(2)}) %copy-start.2) | copy-done | bytes 120
  3.3 0.8 %shard_map.46 = (bf16[48,1024]{1,0:T(8,128)(2,1)S(1)}, bf16[1024,256]{1,0:T(8,128)(2,1)S(1)}) custom-call(s32[3,8]{1,0:T(4,128)S(1)} %copy-done.2, s32[2,8]{1,0:T(2,128)S(1)} %bitcast.1, bf16[48,1024]{1,0:T(8,128)(2,1)S(1)} %copy-done.1, bf16[1024,256]{1,0:T(8,128)(2,1)S(1)} %copy-done), custom_call_target="tpu_custom_call" | custom-call | tf_op jit(solution)/shard_map/pallas_call | solution.py:61
  4.1 3.0 %collective-permute-start.8 = (bf16[1024,256]{1,0:T(8,128)(2,1)S(1)}, bf16[1024,256]{1,0:T(8,128)(2,1)S(1)}, u32[]{:S(2)}, u32[]{:S(2)}) collective-permute-start(bf16[1024,256]{1,0:T(8,128)(2,1)S(1)} %get-tuple-element.17.refs_8_), channel_id=1, source_target_pairs={{0,16},{8,24},{16,0},{24,8},{1,17},{9,25},{17,1},{25,9},{2,18},{10... | collective-permute-start | bytes 1572872 | tf_op jit(solution)/shard_map/ppermute | solution.py:70
  7.1 1.5 %collective-permute-start.2 = (bf16[48,1024]{1,0:T(8,128)(2,1)S(1)}, bf16[48,1024]{1,0:T(8,128)(2,1)S(1)}, u32[]{:S(2)}, u32[]{:S(2)}) collective-permute-start(bf16[48,1024]{1,0:T(8,128)(2,1)S(1)} %get-tuple-element.12.refs_0_), channel_id=1, source_target_pairs={{0,1},{1,0},{2,3},{3,2},{4,5},{5,4},{6,7},{7,6},{8,9},{9,8},{10,11... | collective-permute-start | bytes 294920 | tf_op jit(solution)/shard_map/ppermute | solution.py:70
  8.6 1.6 %collective-permute-start.1 = (bf16[48,1024]{1,0:T(8,128)(2,1)S(1)}, bf16[48,1024]{1,0:T(8,128)(2,1)S(1)}, u32[]{:S(2)}, u32[]{:S(2)}) collective-permute-start(bf16[48,1024]{1,0:T(8,128)(2,1)S(1)} %get-tuple-element.12.refs_0_), channel_id=1, source_target_pairs={{0,2},{1,3},{2,0},{3,1},{4,6},{5,7},{6,4},{7,5},{8,10},{9,11},{10,... | collective-permute-start | bytes 294920 | tf_op jit(solution)/shard_map/ppermute | solution.py:70
  10.2 2.6 %collective-permute-start = (bf16[48,1024]{1,0:T(8,128)(2,1)S(1)}, bf16[48,1024]{1,0:T(8,128)(2,1)S(1)}, u32[]{:S(2)}, u32[]{:S(2)}) collective-permute-start(bf16[48,1024]{1,0:T(8,128)(2,1)S(1)} %get-tuple-element.12.refs_0_), channel_id=1, source_target_pairs={{0,4},{1,5},{2,6},{3,7},{4,0},{5,1},{6,2},{7,3},{8,12},{9,13},{10,... | collective-permute-start | bytes 294920 | tf_op jit(solution)/shard_map/ppermute | solution.py:70
  12.8 0.0 collective-permute-done.2.refs_1_
  12.8 1.4 %collective-permute-done.1.refs_2_ = bf16[48,1024]{1,0:T(8,128)(2,1)S(1)} collective-permute-done((bf16[48,1024]{1,0:T(8,128)(2,1)S(1)}, bf16[48,1024]{1,0:T(8,128)(2,1)S(1)}, u32[]{:S(2)}, u32[]{:S(2)}) %collective-permute-start.1) | collective-permute-done | bytes 98336 | tf_op jit(solution)/shard_map/ppermute | solution.py:70
  14.2 2.7 %collective-permute-done.refs_4_ = bf16[48,1024]{1,0:T(8,128)(2,1)S(1)} collective-permute-done((bf16[48,1024]{1,0:T(8,128)(2,1)S(1)}, bf16[48,1024]{1,0:T(8,128)(2,1)S(1)}, u32[]{:S(2)}, u32[]{:S(2)}) %collective-permute-start) | collective-permute-done | bytes 98336 | tf_op jit(solution)/shard_map/ppermute | solution.py:70
  16.9 0.5 %collective-permute-start.5 = (bf16[48,1024]{1,0:T(8,128)(2,1)S(1)}, bf16[48,1024]{1,0:T(8,128)(2,1)S(1)}, u32[]{:S(2)}, u32[]{:S(2)}) collective-permute-start(bf16[48,1024]{1,0:T(8,128)(2,1)S(1)} %collective-permute-done.refs_4_), channel_id=1, source_target_pairs={{0,2},{1,3},{2,0},{3,1},{4,6},{5,7},{6,4},{7,5},{8,10},{9,11},{10,... | collective-permute-start | bytes 294920 | tf_op jit(solution)/shard_map/ppermute | solution.py:70
  17.4 0.5 %collective-permute-start.3 = (bf16[48,1024]{1,0:T(8,128)(2,1)S(1)}, bf16[48,1024]{1,0:T(8,128)(2,1)S(1)}, u32[]{:S(2)}, u32[]{:S(2)}) collective-permute-start(bf16[48,1024]{1,0:T(8,128)(2,1)S(1)} %collective-permute-done.1.refs_2_), channel_id=1, source_target_pairs={{0,1},{1,0},{2,3},{3,2},{4,5},{5,4},{6,7},{7,6},{8,9},{9,8},{10,11... | collective-permute-start | bytes 294920 | tf_op jit(solution)/shard_map/ppermute | solution.py:70
  17.9 2.5 %collective-permute-start.6 = (bf16[48,1024]{1,0:T(8,128)(2,1)S(1)}, bf16[48,1024]{1,0:T(8,128)(2,1)S(1)}, u32[]{:S(2)}, u32[]{:S(2)}) collective-permute-start(bf16[48,1024]{1,0:T(8,128)(2,1)S(1)} %collective-permute-done.refs_4_), channel_id=1, source_target_pairs={{0,3},{1,2},{2,1},{3,0},{4,7},{5,6},{6,5},{7,4},{8,11},{9,10},{10,... | collective-permute-start | bytes 294920 | tf_op jit(solution)/shard_map/ppermute | solution.py:70
  20.4 0.5 %collective-permute-start.4 = (bf16[48,1024]{1,0:T(8,128)(2,1)S(1)}, bf16[48,1024]{1,0:T(8,128)(2,1)S(1)}, u32[]{:S(2)}, u32[]{:S(2)}) collective-permute-start(bf16[48,1024]{1,0:T(8,128)(2,1)S(1)} %collective-permute-done.refs_4_), channel_id=1, source_target_pairs={{0,1},{1,0},{2,3},{3,2},{4,5},{5,4},{6,7},{7,6},{8,9},{9,8},{10,11... | collective-permute-start | bytes 294920 | tf_op jit(solution)/shard_map/ppermute | solution.py:70
  20.9 0.6 %collective-permute-done.5.refs_6_ = bf16[48,1024]{1,0:T(8,128)(2,1)S(1)} collective-permute-done((bf16[48,1024]{1,0:T(8,128)(2,1)S(1)}, bf16[48,1024]{1,0:T(8,128)(2,1)S(1)}, u32[]{:S(2)}, u32[]{:S(2)}) %collective-permute-start.5) | collective-permute-done | bytes 98336 | tf_op jit(solution)/shard_map/ppermute | solution.py:70
  21.5 0.0 collective-permute-start.7
  21.5 0.5 %collective-permute-done.3.refs_3_ = bf16[48,1024]{1,0:T(8,128)(2,1)S(1)} collective-permute-done((bf16[48,1024]{1,0:T(8,128)(2,1)S(1)}, bf16[48,1024]{1,0:T(8,128)(2,1)S(1)}, u32[]{:S(2)}, u32[]{:S(2)}) %collective-permute-start.3) | collective-permute-done | bytes 98336 | tf_op jit(solution)/shard_map/ppermute | solution.py:70
  22.0 1.4 %collective-permute-done.6.refs_7_ = bf16[48,1024]{1,0:T(8,128)(2,1)S(1)} collective-permute-done((bf16[48,1024]{1,0:T(8,128)(2,1)S(1)}, bf16[48,1024]{1,0:T(8,128)(2,1)S(1)}, u32[]{:S(2)}, u32[]{:S(2)}) %collective-permute-start.6) | collective-permute-done | bytes 98336 | tf_op jit(solution)/shard_map/ppermute | solution.py:70
  23.4 1.6 %collective-permute-done.4.refs_5_ = bf16[48,1024]{1,0:T(8,128)(2,1)S(1)} collective-permute-done((bf16[48,1024]{1,0:T(8,128)(2,1)S(1)}, bf16[48,1024]{1,0:T(8,128)(2,1)S(1)}, u32[]{:S(2)}, u32[]{:S(2)}) %collective-permute-start.4) | collective-permute-done | bytes 98336 | tf_op jit(solution)/shard_map/ppermute | solution.py:70
  25.0 0.0 collective-permute-done.8.refs_10_
  25.0 0.0 collective-permute-start.9
  25.0 0.0 collective-permute-done.7.refs_9_
  25.0 1.9 %collective-permute-done.9.refs_11_ = bf16[1024,256]{1,0:T(8,128)(2,1)S(1)} collective-permute-done((bf16[1024,256]{1,0:T(8,128)(2,1)S(1)}, bf16[1024,256]{1,0:T(8,128)(2,1)S(1)}, u32[]{:S(2)}, u32[]{:S(2)}) %collective-permute-start.9) | collective-permute-done | bytes 524320 | tf_op jit(solution)/shard_map/ppermute | solution.py:70
  26.9 1.8 %shard_map.47 = bf16[384,1024]{1,0:T(8,128)(2,1)} custom-call(bf16[48,1024]{1,0:T(8,128)(2,1)S(1)} %get-tuple-element.12.refs_0_, bf16[48,1024]{1,0:T(8,128)(2,1)S(1)} %collective-permute-done.2.refs_1_, bf16[48,1024]{1,0:T(8,128)(2,1)S(1)} %collective-permute-done.1.refs_2_, bf16[48,1024]{1,0:T(8,128)(2,1)S(1)} %collective-permute-done.3.refs_3_, ...), custom_call_target="tpu_custom_call" | custom-call | tf_op jit(solution)/shard_map/pallas_call | solution.py:87
Async XLA Ops:
  0.0 0.7 %copy-start.3 = (s32[8,2]{0,1:T(2,128)S(1)}, s32[8,2]{0,1:T(2,128)}, u32[]{:S(2)}) copy-start(s32[8,2]{0,1:T(2,128)} %param.7) | copy-start | bytes 196
  0.7 1.0 %copy-start = (bf16[1024,256]{1,0:T(8,128)(2,1)S(1)}, bf16[1024,256]{1,0:T(8,128)(2,1)}, u32[]{:S(2)}) copy-start(bf16[1024,256]{1,0:T(8,128)(2,1)} %b.1) | copy-start | bytes 1572868
  1.7 0.9 %copy-start.1 = (bf16[48,1024]{1,0:T(8,128)(2,1)S(1)}, bf16[48,1024]{1,0:T(8,128)(2,1)}, u32[]{:S(2)}) copy-start(bf16[48,1024]{1,0:T(8,128)(2,1)} %a.1) | copy-start | bytes 294916
  2.6 0.7 %copy-start.2 = (s32[3,8]{1,0:T(4,128)S(1)}, s32[3,8]{1,0:T(4,128)}, u32[]{:S(2)}) copy-start(s32[3,8]{1,0:T(4,128)} %amask.1) | copy-start | bytes 292
  4.1 20.9 %collective-permute-start.8 = (bf16[1024,256]{1,0:T(8,128)(2,1)S(1)}, bf16[1024,256]{1,0:T(8,128)(2,1)S(1)}, u32[]{:S(2)}, u32[]{:S(2)}) collective-permute-start(bf16[1024,256]{1,0:T(8,128)(2,1)S(1)} %get-tuple-element.17.refs_8_), channel_id=1, source_target_pairs={{0,16},{8,24},{16,0},{24,8},{1,17},{9,25},{17,1},{25,9},{2,18},{10... | collective-permute-start | bytes 1572872 | tf_op jit(solution)/shard_map/ppermute | solution.py:70
  7.1 5.7 %collective-permute-start.2 = (bf16[48,1024]{1,0:T(8,128)(2,1)S(1)}, bf16[48,1024]{1,0:T(8,128)(2,1)S(1)}, u32[]{:S(2)}, u32[]{:S(2)}) collective-permute-start(bf16[48,1024]{1,0:T(8,128)(2,1)S(1)} %get-tuple-element.12.refs_0_), channel_id=1, source_target_pairs={{0,1},{1,0},{2,3},{3,2},{4,5},{5,4},{6,7},{7,6},{8,9},{9,8},{10,11... | collective-permute-start | bytes 294920 | tf_op jit(solution)/shard_map/ppermute | solution.py:70
  8.6 5.6 %collective-permute-start.1 = (bf16[48,1024]{1,0:T(8,128)(2,1)S(1)}, bf16[48,1024]{1,0:T(8,128)(2,1)S(1)}, u32[]{:S(2)}, u32[]{:S(2)}) collective-permute-start(bf16[48,1024]{1,0:T(8,128)(2,1)S(1)} %get-tuple-element.12.refs_0_), channel_id=1, source_target_pairs={{0,2},{1,3},{2,0},{3,1},{4,6},{5,7},{6,4},{7,5},{8,10},{9,11},{10,... | collective-permute-start | bytes 294920 | tf_op jit(solution)/shard_map/ppermute | solution.py:70
  10.2 6.7 %collective-permute-start = (bf16[48,1024]{1,0:T(8,128)(2,1)S(1)}, bf16[48,1024]{1,0:T(8,128)(2,1)S(1)}, u32[]{:S(2)}, u32[]{:S(2)}) collective-permute-start(bf16[48,1024]{1,0:T(8,128)(2,1)S(1)} %get-tuple-element.12.refs_0_), channel_id=1, source_target_pairs={{0,4},{1,5},{2,6},{3,7},{4,0},{5,1},{6,2},{7,3},{8,12},{9,13},{10,... | collective-permute-start | bytes 294920 | tf_op jit(solution)/shard_map/ppermute | solution.py:70
  16.9 4.6 %collective-permute-start.5 = (bf16[48,1024]{1,0:T(8,128)(2,1)S(1)}, bf16[48,1024]{1,0:T(8,128)(2,1)S(1)}, u32[]{:S(2)}, u32[]{:S(2)}) collective-permute-start(bf16[48,1024]{1,0:T(8,128)(2,1)S(1)} %collective-permute-done.refs_4_), channel_id=1, source_target_pairs={{0,2},{1,3},{2,0},{3,1},{4,6},{5,7},{6,4},{7,5},{8,10},{9,11},{10,... | collective-permute-start | bytes 294920 | tf_op jit(solution)/shard_map/ppermute | solution.py:70
  17.4 4.6 %collective-permute-start.3 = (bf16[48,1024]{1,0:T(8,128)(2,1)S(1)}, bf16[48,1024]{1,0:T(8,128)(2,1)S(1)}, u32[]{:S(2)}, u32[]{:S(2)}) collective-permute-start(bf16[48,1024]{1,0:T(8,128)(2,1)S(1)} %collective-permute-done.1.refs_2_), channel_id=1, source_target_pairs={{0,1},{1,0},{2,3},{3,2},{4,5},{5,4},{6,7},{7,6},{8,9},{9,8},{10,11... | collective-permute-start | bytes 294920 | tf_op jit(solution)/shard_map/ppermute | solution.py:70
  17.9 5.5 %collective-permute-start.6 = (bf16[48,1024]{1,0:T(8,128)(2,1)S(1)}, bf16[48,1024]{1,0:T(8,128)(2,1)S(1)}, u32[]{:S(2)}, u32[]{:S(2)}) collective-permute-start(bf16[48,1024]{1,0:T(8,128)(2,1)S(1)} %collective-permute-done.refs_4_), channel_id=1, source_target_pairs={{0,3},{1,2},{2,1},{3,0},{4,7},{5,6},{6,5},{7,4},{8,11},{9,10},{10,... | collective-permute-start | bytes 294920 | tf_op jit(solution)/shard_map/ppermute | solution.py:70
  20.4 4.6 %collective-permute-start.4 = (bf16[48,1024]{1,0:T(8,128)(2,1)S(1)}, bf16[48,1024]{1,0:T(8,128)(2,1)S(1)}, u32[]{:S(2)}, u32[]{:S(2)}) collective-permute-start(bf16[48,1024]{1,0:T(8,128)(2,1)S(1)} %collective-permute-done.refs_4_), channel_id=1, source_target_pairs={{0,1},{1,0},{2,3},{3,2},{4,5},{5,4},{6,7},{7,6},{8,9},{9,8},{10,11... | collective-permute-start | bytes 294920 | tf_op jit(solution)/shard_map/ppermute | solution.py:70
  21.5 3.5 %collective-permute-start.7 = (bf16[1024,256]{1,0:T(8,128)(2,1)S(1)}, bf16[1024,256]{1,0:T(8,128)(2,1)S(1)}, u32[]{:S(2)}, u32[]{:S(2)}) collective-permute-start(bf16[1024,256]{1,0:T(8,128)(2,1)S(1)} %get-tuple-element.17.refs_8_), channel_id=1, source_target_pairs={{0,8},{8,0},{16,24},{24,16},{1,9},{9,1},{17,25},{25,17},{2,10},{10... | collective-permute-start | bytes 1572872 | tf_op jit(solution)/shard_map/ppermute | solution.py:70
  25.0 1.9 %collective-permute-start.9 = (bf16[1024,256]{1,0:T(8,128)(2,1)S(1)}, bf16[1024,256]{1,0:T(8,128)(2,1)S(1)}, u32[]{:S(2)}, u32[]{:S(2)}) collective-permute-start(bf16[1024,256]{1,0:T(8,128)(2,1)S(1)} %collective-permute-done.8.refs_10_), channel_id=1, source_target_pairs={{0,8},{8,0},{16,24},{24,16},{1,9},{9,1},{17,25},{25,17},{2,10},{10... | collective-permute-start | bytes 1572872 | tf_op jit(solution)/shard_map/ppermute | solution.py:70

commit v2 on v1

v2 whole, which is shorter than its diff:
```python
import functools
import jax
import jax.numpy as jnp
from jax import lax
from jax.experimental import pallas as pl
from jax.experimental.pallas import tpu as pltpu
from jax.sharding import PartitionSpec as P

TILE = 128
OTILE = 16
VMEM = pl.BlockSpec(memory_space=pltpu.VMEM)
SMEM = pl.BlockSpec(memory_space=pltpu.SMEM)
ANY = pl.BlockSpec(memory_space=pl.ANY)


def limit(*values):
    nbytes = sum(v.size * v.dtype.itemsize for v in values)
    return pltpu.CompilerParams(vmem_limit_bytes=2 * nbytes + 4 * 2**20)


def after(v, *deps):
    return lax.optimization_barrier((v, *deps))[0]


def held(v):
    return pltpu.with_memory_space_constraint(v, pltpu.VMEM)


def mask_kernel(amask, bmask, a, b, a_out, b_out):
    def factor(mask, i, j):
        return mask[i, j].astype(jnp.float32).astype(a.dtype)

    for i in range(a.shape[0] // OTILE):
        for j in range(a.shape[1] // TILE):
            at = (slice(i * OTILE, (i + 1) * OTILE), slice(j * TILE, (j + 1) * TILE))
            a_out[at] = a[at] * factor(amask, i, j)
    for i in range(b.shape[0] // TILE):
        for j in range(b.shape[1] // TILE):
            at = (slice(i * TILE, (i + 1) * TILE), slice(j * TILE, (j + 1) * TILE))
            b_out[at] = b[at] * factor(bmask, j, i)


def product(a, b, dtype):
    return (0.5 * jnp.dot(a, b, preferred_element_type=jnp.float32)).astype(dtype)


def near_kernel(masks, *refs):
    a_refs, b_refs, (a_all, near) = refs[: len(masks)], refs[len(masks) : -2], refs[-2:]
    for ks, ref in zip(masks, a_refs, strict=True):
        rows = ref.shape[0] // len(ks)
        for i, k in enumerate(ks):
            at = pl.multiple_of((lax.axis_index("grp") ^ k) * rows, OTILE)
            a_all[pl.ds(at, rows), :] = ref[i * rows : (i + 1) * rows, :]
    for n, b in enumerate(b_refs):
        near[n] = product(a_all[...], b[...], near.dtype)


def far_kernel(near_at, far_at, a_all, near, *refs):
    b_refs, (out, stage, near_sems, far_sems) = refs[:-4], refs[-4:]
    rows, width = near.shape[1:]

    def write(block, k, top, sem):
        at = pl.multiple_of((lax.axis_index("blk") ^ k) * width, TILE)
        copy = pltpu.make_async_copy(block, out.at[pl.ds(top, block.shape[0]), pl.ds(at, width)], sem)
        copy.start()
        return copy

    copies = [write(near.at[n], k, 0, near_sems.at[n]) for n, k in enumerate(near_at)]
    cuts = far_sems.shape[1]
    for n, k in enumerate(far_at):
        for c in range(cuts):
            at = pl.ds(c * (rows // cuts), rows // cuts)
            stage[n, at, :] = product(a_all[at, :], b_refs[n][...], stage.dtype)
            copies.append(write(stage.at[n, at], k, c * (rows // cuts), far_sems.at[n, c]))
    for copy in copies:
        copy.wait()


def local(n_blk, n_grp, a, b, amask, bmask):
    a_own, b_own = pl.pallas_call(
        mask_kernel,
        out_shape=[pltpu.VMEM(a.shape, a.dtype), pltpu.VMEM(b.shape, b.dtype)],
        in_specs=[SMEM, SMEM, VMEM, VMEM],
        out_specs=[VMEM, VMEM],
        compiler_params=pltpu.CompilerParams(vmem_limit_bytes=56 * 2**20),
    )(amask, bmask.T, a, b)

    def swap(v, axis, n, k):
        return lax.ppermute(v, axis, [(i, i ^ k) for i in range(n)])

    def joined(*vs):
        def join_kernel(*refs):
            top = 0
            for ref in refs[:-1]:
                refs[-1][top : top + ref.shape[0], :] = ref[...]
                top += ref.shape[0]

        rows = sum(v.shape[0] for v in vs)
        return pl.pallas_call(
            join_kernel,
            out_shape=pltpu.VMEM((rows, vs[0].shape[1]), vs[0].dtype),
            in_specs=[VMEM] * len(vs),
            out_specs=VMEM,
            compiler_params=limit(*vs),
        )(*[held(v) for v in vs])

    def line(*vs):
        done = []
        for v in vs:
            done = list(lax.optimization_barrier((v, *done)))
        return done[::-1]

    def along_grp(v, k):
        return swap(v, "grp", n_grp, k)

    def along_blk(v, k):
        return swap(v, "blk", n_blk, k)

    panels = {0: b_own} | {k: along_blk(b_own, k) for k in range(2, n_blk, 2)}
    z4, z2, z1 = along_grp(a_own, 4), along_grp(a_own, 2), along_grp(a_own, 1)
    z4, z2 = line(z4, z2)
    pair = joined(z2, z4)
    m7 = along_grp(z4, 3)
    m35 = along_grp(after(pair, z1), 1)
    m6 = along_grp(after(z4, z1), 2)
    panels |= {k ^ 1: along_blk(after(v, z1), 1) for k, v in panels.items()}
    m7, m35, m6 = line(m7, m35, m6)
    shards = {(0,): a_own, (1,): z1, (2,): z2, (3, 5): m35, (4,): z4, (6,): m6, (7,): m7}
    for top in [8 << i for i in range((n_grp // 8).bit_length() - 1)]:
        shards[(top,)] = along_grp(a_own, top)
        shards |= {(top ^ k,): along_grp(shards[(top,)], k) for k in range(1, top)}
    rows, depth, width = a.shape[0] * n_grp, a.shape[1], b.shape[1]
    out = jax.ShapeDtypeStruct((rows, width * n_blk), a.dtype)
    near_at, far_at = list(range(0, n_blk, 2)), list(range(1, n_blk, 2))
    a_full, near = pl.pallas_call(
        functools.partial(near_kernel, list(shards)),
        out_shape=[pltpu.VMEM((rows, depth), a.dtype), pltpu.VMEM((len(near_at), rows, width), a.dtype)],
        in_specs=[VMEM] * (len(shards) + len(near_at)),
        out_specs=[VMEM, VMEM],
        compiler_params=limit(out),
        cost_estimate=pl.CostEstimate(flops=50 * 10**8, bytes_accessed=2**22, transcendentals=0),
    )(*[held(v) for v in [*shards.values()] + [panels[k] for k in near_at]])
    return pl.pallas_call(
        functools.partial(far_kernel, near_at, far_at),
        out_shape=out,
        in_specs=[VMEM] * (2 + len(far_at)),
        out_specs=ANY,
        scratch_shapes=[
            pltpu.VMEM((len(far_at), rows, width), a.dtype),
            pltpu.SemaphoreType.DMA((len(near_at),)),
            pltpu.SemaphoreType.DMA((len(far_at), 2)),
        ],
        compiler_params=limit(out),
    )(*[held(v) for v in [a_full, near] + [panels[k] for k in far_at]])


def solution(mesh):
    return jax.shard_map(
        functools.partial(local, mesh.shape["blk"], mesh.shape["grp"]),
        mesh=mesh,
        in_specs=(
            P(("blk", "grp"), None),
            P(None, ("grp", "blk")),
            P(("blk", "grp"), None),
            P(None, ("grp", "blk")),
        ),
        out_specs=P("blk", "grp"),
        check_vma=False,
    )
```

time: 28.9 us -> 22.4 us (0.78)
  waiting for transfers between devices: 10.1 us -> 6.26 us
  local copies, waits for them, and re-layouts: 3.29 us -> 0 us
  Pallas kernels: 2.55 us -> 3.22 us
    ppermute x10 -> x9, waiting for transfers between devices: 10.1 us -> 6.26 us  [swap(): return lax.ppermute(v, axis, [(i, i ^ k) for i in range(n)])]
    unnamed x8 -> x0, local copies, waits for them, and re-layouts: 3.29 us -> none
    pallas_call x1, Pallas kernels: 0.75 us -> 1.29 us  [local(): pl.pallas_call(mask_kernel, out_shape=[pltpu.VMEM(a.shape, a.dtype), pltp...]
    pallas_call x1 -> x3, Pallas kernels: 1.79 us -> 1.93 us  [the longest x1 1.31 us: local(): pl.pallas_call(functools.partial(far_kernel, near_at, far_at), out_shape=...]
    ppermute x10 -> x9, starting transfers between devices: 12.7 us -> 12.7 us  [swap(): return lax.ppermute(v, axis, [(i, i ^ k) for i in range(n)])]
  transfers between devices with their start and end apart: 10 -> 9, of which waited for: 7 -> 5; matrix products, arithmetic and copies ran while one was open for 0% -> 0% of each run, Pallas kernels for 0% -> 3%
where the time goes in v2:
time: 22.4 us; the launch traced here: 22.2 us
  starting transfers between devices  12.7 us (57%)
  waiting for transfers between devices  6.26 us (28%)
  Pallas kernels  3.22 us (14%)
    ppermute x9, starting transfers between devices, swap(): return lax.ppermute(v, axis, [(i, i ^ k) for i in range(n)])  12.7 us
    ppermute x9, waiting for transfers between devices, swap(): return lax.ppermute(v, axis, [(i, i ^ k) for i in range(n)])  6.26 us
    pallas_call x1, Pallas kernels, local(): pl.pallas_call(functools.partial(far_kernel, near_at, far_at), out_shape=...  1.31 us
    pallas_call x1, Pallas kernels, local(): pl.pallas_call(mask_kernel, out_shape=[pltpu.VMEM(a.shape, a.dtype), pltp...  1.29 us
    pallas_call x1, Pallas kernels, local(): pl.pallas_call(functools.partial(near_kernel, list(shards)), out_shape=[p...  0.6 us
  transfers between devices with their start and end apart: 9, of which 5 were waited for; matrix products, arithmetic and copies ran while one was open for 0% of the time, Pallas kernels for 3%

profile of v2, /device:TPU:0, one launch (start us, length us, event | category | flops | bytes accessed | tf_op | source)
XLA Modules:
  0.0 22.2 jit_solution(13440531095507742368)
XLA Ops:
  0.0 1.3 %shard_map.46 = (bf16[48,1024]{1,0:T(8,128)(2,1)S(1)}, bf16[1024,256]{1,0:T(8,128)(2,1)S(1)}) custom-call(s32[3,8]{1,0:T(4,128)} %amask.1, s32[2,8]{1,0:T(2,128)} %bitcast.1, bf16[48,1024]{1,0:T(8,128)(2,1)} %a.1, bf16[1024,256]{1,0:T(8,128)(2,1)} %b.1), custom_call_target="tpu_custom_call" | custom-call | tf_op jit(solution)/shard_map/pallas_call | solution.py:80
  1.3 3.0 %collective-permute-start.6 = (bf16[1024,256]{1,0:T(8,128)(2,1)S(1)}, bf16[1024,256]{1,0:T(8,128)(2,1)S(1)}, u32[]{:S(2)}, u32[]{:S(2)}) collective-permute-start(bf16[1024,256]{1,0:T(8,128)(2,1)S(1)} %get-tuple-element.33.refs_7_), channel_id=1, source_target_pairs={{0,16},{8,24},{16,0},{24,8},{1,17},{9,25},{17,1},{25,9},{2,18},{10... | collective-permute-start | bytes 1572872 | tf_op jit(solution)/shard_map/ppermute | solution.py:89
  4.3 2.6 %collective-permute-start.2 = (bf16[48,1024]{1,0:T(8,128)(2,1)S(1)}, bf16[48,1024]{1,0:T(8,128)(2,1)S(1)}, u32[]{:S(2)}, u32[]{:S(2)}) collective-permute-start(bf16[48,1024]{1,0:T(8,128)(2,1)S(1)} %get-tuple-element.20.refs_0_), channel_id=1, source_target_pairs={{0,4},{1,5},{2,6},{3,7},{4,0},{5,1},{6,2},{7,3},{8,12},{9,13},{10,... | collective-permute-start | bytes 294920 | tf_op jit(solution)/shard_map/ppermute | solution.py:89
  6.9 1.6 %collective-permute-start.1 = (bf16[48,1024]{1,0:T(8,128)(2,1)S(1)}, bf16[48,1024]{1,0:T(8,128)(2,1)S(1)}, u32[]{:S(2)}, u32[]{:S(2)}) collective-permute-start(bf16[48,1024]{1,0:T(8,128)(2,1)S(1)} %get-tuple-element.20.refs_0_), channel_id=1, source_target_pairs={{0,2},{1,3},{2,0},{3,1},{4,6},{5,7},{6,4},{7,5},{8,10},{9,11},{10,... | collective-permute-start | bytes 294920 | tf_op jit(solution)/shard_map/ppermute | solution.py:89
  8.5 1.5 %collective-permute-start = (bf16[48,1024]{1,0:T(8,128)(2,1)S(1)}, bf16[48,1024]{1,0:T(8,128)(2,1)S(1)}, u32[]{:S(2)}, u32[]{:S(2)}) collective-permute-start(bf16[48,1024]{1,0:T(8,128)(2,1)S(1)} %get-tuple-element.20.refs_0_), channel_id=1, source_target_pairs={{0,1},{1,0},{2,3},{3,2},{4,5},{5,4},{6,7},{7,6},{8,9},{9,8},{10,11... | collective-permute-start | bytes 294920 | tf_op jit(solution)/shard_map/ppermute | solution.py:89
  10.0 1.6 %collective-permute-done.2.refs_1_.refs_4_ = bf16[48,1024]{1,0:T(8,128)(2,1)S(1)} collective-permute-done((bf16[48,1024]{1,0:T(8,128)(2,1)S(1)}, bf16[48,1024]{1,0:T(8,128)(2,1)S(1)}, u32[]{:S(2)}, u32[]{:S(2)}) %collective-permute-start.2) | collective-permute-done | bytes 98336 | tf_op jit(solution)/shard_map/ppermute | solution.py:89
  11.6 0.4 %collective-permute-done.1.refs_0_.refs_2_ = bf16[48,1024]{1,0:T(8,128)(2,1)S(1)} collective-permute-done((bf16[48,1024]{1,0:T(8,128)(2,1)S(1)}, bf16[48,1024]{1,0:T(8,128)(2,1)S(1)}, u32[]{:S(2)}, u32[]{:S(2)}) %collective-permute-start.1) | collective-permute-done | bytes 98336 | tf_op jit(solution)/shard_map/ppermute | solution.py:89
  11.9 1.1 %collective-permute-done.refs_1_ = bf16[48,1024]{1,0:T(8,128)(2,1)S(1)} collective-permute-done((bf16[48,1024]{1,0:T(8,128)(2,1)S(1)}, bf16[48,1024]{1,0:T(8,128)(2,1)S(1)}, u32[]{:S(2)}, u32[]{:S(2)}) %collective-permute-start) | collective-permute-done | bytes 98336 | tf_op jit(solution)/shard_map/ppermute | solution.py:89
  13.1 1.5 %collective-permute-start.4 = (bf16[96,1024]{1,0:T(8,128)(2,1)S(1)}, bf16[96,1024]{1,0:T(8,128)(2,1)S(1)}, u32[]{:S(2)}, u32[]{:S(2)}) collective-permute-start(bf16[96,1024]{1,0:T(8,128)(2,1)S(1)} %shard_map.47), channel_id=1, source_target_pairs={{0,1},{1,0},{2,3},{3,2},{4,5},{5,4},{6,7},{7,6},{8,9},{9,8},{10,11... | collective-permute-start | bytes 589832 | tf_op jit(solution)/shard_map/ppermute | solution.py:89
  14.6 0.4 %collective-permute-start.5 = (bf16[48,1024]{1,0:T(8,128)(2,1)S(1)}, bf16[48,1024]{1,0:T(8,128)(2,1)S(1)}, u32[]{:S(2)}, u32[]{:S(2)}) collective-permute-start(bf16[48,1024]{1,0:T(8,128)(2,1)S(1)} %collective-permute-done.2.refs_1_.refs_4_), channel_id=1, source_target_pairs={{0,3},{1,2},{2,1},{3,0},{4,7},{5,6},{6,5},{7,4},{8,11},{9,10},{10,... | collective-permute-start | bytes 294920 | tf_op jit(solution)/shard_map/ppermute | solution.py:89
  15.1 1.5 %collective-permute-start.3 = (bf16[48,1024]{1,0:T(8,128)(2,1)S(1)}, bf16[48,1024]{1,0:T(8,128)(2,1)S(1)}, u32[]{:S(2)}, u32[]{:S(2)}) collective-permute-start(bf16[48,1024]{1,0:T(8,128)(2,1)S(1)} %collective-permute-done.2.refs_1_.refs_4_), channel_id=1, source_target_pairs={{0,2},{1,3},{2,0},{3,1},{4,6},{5,7},{6,4},{7,5},{8,10},{9,11},{10,... | collective-permute-start | bytes 294920 | tf_op jit(solution)/shard_map/ppermute | solution.py:89
  16.6 0.0 collective-permute-start.7
  16.6 0.0 collective-permute-done.6.refs_8_
  16.6 0.5 %collective-permute-start.8 = (bf16[1024,256]{1,0:T(8,128)(2,1)S(1)}, bf16[1024,256]{1,0:T(8,128)(2,1)S(1)}, u32[]{:S(2)}, u32[]{:S(2)}) collective-permute-start(bf16[1024,256]{1,0:T(8,128)(2,1)S(1)} %collective-permute-done.6.refs_8_), channel_id=1, source_target_pairs={{0,8},{8,0},{16,24},{24,16},{1,9},{9,1},{17,25},{25,17},{2,10},{10... | collective-permute-start | bytes 1572872 | tf_op jit(solution)/shard_map/ppermute | solution.py:89
  17.1 3.1 %collective-permute-done.5.refs_6_ = bf16[48,1024]{1,0:T(8,128)(2,1)S(1)} collective-permute-done((bf16[48,1024]{1,0:T(8,128)(2,1)S(1)}, bf16[48,1024]{1,0:T(8,128)(2,1)S(1)}, u32[]{:S(2)}, u32[]{:S(2)}) %collective-permute-start.5) | collective-permute-done | bytes 98336 | tf_op jit(solution)/shard_map/ppermute | solution.py:89
  20.2 0.0 collective-permute-done.4.refs_3_
  20.2 0.1 collective-permute-done.3.refs_5_
  20.3 0.6 %shard_map.48 = (bf16[384,1024]{1,0:T(8,128)(2,1)S(1)}, bf16[2,384,256]{2,1,0:T(8,128)(2,1)S(1)}) custom-call(bf16[48,1024]{1,0:T(8,128)(2,1)S(1)} %get-tuple-element.20.refs_0_, bf16[48,1024]{1,0:T(8,128)(2,1)S(1)} %collective-permute-done.refs_1_, bf16[48,1024]{1,0:T(8,128)(2,1)S(1)} %collective-permute-done.1.refs_0_.refs_2_, ...), custom_call_target="tpu_custom_call" | custom-call | flops 5000000000 | bytes 4194304 | tf_op jit(solution)/shard_map/pallas_call | solution.py:135
  20.9 0.0 collective-permute-done.7.refs_0_
  20.9 0.0 collective-permute-done.8.refs_1_
  20.9 1.3 %shard_map.49 = bf16[384,1024]{1,0:T(8,128)(2,1)} custom-call(bf16[384,1024]{1,0:T(8,128)(2,1)S(1)} %get-tuple-element.31.a_all, bf16[2,384,256]{2,1,0:T(8,128)(2,1)S(1)} %get-tuple-element.32.near, bf16[1024,256]{1,0:T(8,128)(2,1)S(1)} %collective-permute-done.7.refs_0_, bf16[1024,256]{1,0:T(8,128)(2,1)S(1)} %collective-permute-done.8.refs_1_), custom_call_target="tpu_custom_call" | custom-call | tf_op jit(solution)/shard_map/pallas_call | solution.py:143
  (1 shorter events, 0.0 us)
Async XLA Ops:
  1.3 15.3 %collective-permute-start.6 = (bf16[1024,256]{1,0:T(8,128)(2,1)S(1)}, bf16[1024,256]{1,0:T(8,128)(2,1)S(1)}, u32[]{:S(2)}, u32[]{:S(2)}) collective-permute-start(bf16[1024,256]{1,0:T(8,128)(2,1)S(1)} %get-tuple-element.33.refs_7_), channel_id=1, source_target_pairs={{0,16},{8,24},{16,0},{24,8},{1,17},{9,25},{17,1},{25,9},{2,18},{10... | collective-permute-start | bytes 1572872 | tf_op jit(solution)/shard_map/ppermute | solution.py:89
  4.3 7.3 %collective-permute-start.2 = (bf16[48,1024]{1,0:T(8,128)(2,1)S(1)}, bf16[48,1024]{1,0:T(8,128)(2,1)S(1)}, u32[]{:S(2)}, u32[]{:S(2)}) collective-permute-start(bf16[48,1024]{1,0:T(8,128)(2,1)S(1)} %get-tuple-element.20.refs_0_), channel_id=1, source_target_pairs={{0,4},{1,5},{2,6},{3,7},{4,0},{5,1},{6,2},{7,3},{8,12},{9,13},{10,... | collective-permute-start | bytes 294920 | tf_op jit(solution)/shard_map/ppermute | solution.py:89
  6.9 5.0 %collective-permute-start.1 = (bf16[48,1024]{1,0:T(8,128)(2,1)S(1)}, bf16[48,1024]{1,0:T(8,128)(2,1)S(1)}, u32[]{:S(2)}, u32[]{:S(2)}) collective-permute-start(bf16[48,1024]{1,0:T(8,128)(2,1)S(1)} %get-tuple-element.20.refs_0_), channel_id=1, source_target_pairs={{0,2},{1,3},{2,0},{3,1},{4,6},{5,7},{6,4},{7,5},{8,10},{9,11},{10,... | collective-permute-start | bytes 294920 | tf_op jit(solution)/shard_map/ppermute | solution.py:89
  8.5 4.6 %collective-permute-start = (bf16[48,1024]{1,0:T(8,128)(2,1)S(1)}, bf16[48,1024]{1,0:T(8,128)(2,1)S(1)}, u32[]{:S(2)}, u32[]{:S(2)}) collective-permute-start(bf16[48,1024]{1,0:T(8,128)(2,1)S(1)} %get-tuple-element.20.refs_0_), channel_id=1, source_target_pairs={{0,1},{1,0},{2,3},{3,2},{4,5},{5,4},{6,7},{7,6},{8,9},{9,8},{10,11... | collective-permute-start | bytes 294920 | tf_op jit(solution)/shard_map/ppermute | solution.py:89
  13.1 7.1 %collective-permute-start.4 = (bf16[96,1024]{1,0:T(8,128)(2,1)S(1)}, bf16[96,1024]{1,0:T(8,128)(2,1)S(1)}, u32[]{:S(2)}, u32[]{:S(2)}) collective-permute-start(bf16[96,1024]{1,0:T(8,128)(2,1)S(1)} %shard_map.47), channel_id=1, source_target_pairs={{0,1},{1,0},{2,3},{3,2},{4,5},{5,4},{6,7},{7,6},{8,9},{9,8},{10,11... | collective-permute-start | bytes 589832 | tf_op jit(solution)/shard_map/ppermute | solution.py:89
  14.6 5.6 %collective-permute-start.5 = (bf16[48,1024]{1,0:T(8,128)(2,1)S(1)}, bf16[48,1024]{1,0:T(8,128)(2,1)S(1)}, u32[]{:S(2)}, u32[]{:S(2)}) collective-permute-start(bf16[48,1024]{1,0:T(8,128)(2,1)S(1)} %collective-permute-done.2.refs_1_.refs_4_), channel_id=1, source_target_pairs={{0,3},{1,2},{2,1},{3,0},{4,7},{5,6},{6,5},{7,4},{8,11},{9,10},{10,... | collective-permute-start | bytes 294920 | tf_op jit(solution)/shard_map/ppermute | solution.py:89
  15.1 5.2 %collective-permute-start.3 = (bf16[48,1024]{1,0:T(8,128)(2,1)S(1)}, bf16[48,1024]{1,0:T(8,128)(2,1)S(1)}, u32[]{:S(2)}, u32[]{:S(2)}) collective-permute-start(bf16[48,1024]{1,0:T(8,128)(2,1)S(1)} %collective-permute-done.2.refs_1_.refs_4_), channel_id=1, source_target_pairs={{0,2},{1,3},{2,0},{3,1},{4,6},{5,7},{6,4},{7,5},{8,10},{9,11},{10,... | collective-permute-start | bytes 294920 | tf_op jit(solution)/shard_map/ppermute | solution.py:89
  16.6 4.3 %collective-permute-start.7 = (bf16[1024,256]{1,0:T(8,128)(2,1)S(1)}, bf16[1024,256]{1,0:T(8,128)(2,1)S(1)}, u32[]{:S(2)}, u32[]{:S(2)}) collective-permute-start(bf16[1024,256]{1,0:T(8,128)(2,1)S(1)} %get-tuple-element.33.refs_7_), channel_id=1, source_target_pairs={{0,8},{8,0},{16,24},{24,16},{1,9},{9,1},{17,25},{25,17},{2,10},{10... | collective-permute-start | bytes 1572872 | tf_op jit(solution)/shard_map/ppermute | solution.py:89
  16.6 4.3 %collective-permute-start.8 = (bf16[1024,256]{1,0:T(8,128)(2,1)S(1)}, bf16[1024,256]{1,0:T(8,128)(2,1)S(1)}, u32[]{:S(2)}, u32[]{:S(2)}) collective-permute-start(bf16[1024,256]{1,0:T(8,128)(2,1)S(1)} %collective-permute-done.6.refs_8_), channel_id=1, source_target_pairs={{0,8},{8,0},{16,24},{24,16},{1,9},{9,1},{17,25},{25,17},{2,10},{10... | collective-permute-start | bytes 1572872 | tf_op jit(solution)/shard_map/ppermute | solution.py:89

commit v3 on v2

--- a/solution.py
+++ b/solution.py
@@ -120,8 +120,8 @@
     z4, z2, z1 = along_grp(a_own, 4), along_grp(a_own, 2), along_grp(a_own, 1)
     z4, z2 = line(z4, z2)
     pair = joined(z2, z4)
+    m35 = along_grp(pair, 1)
     m7 = along_grp(z4, 3)
-    m35 = along_grp(after(pair, z1), 1)
     m6 = along_grp(after(z4, z1), 2)
     panels |= {k ^ 1: along_blk(after(v, z1), 1) for k, v in panels.items()}
     m7, m35, m6 = line(m7, m35, m6)

time: 22.4 us -> 21.8 us (0.973)
  starting transfers between devices: 12.7 us -> 12.2 us
    ppermute x9, starting transfers between devices: 12.7 us -> 12.2 us  [swap(): return lax.ppermute(v, axis, [(i, i ^ k) for i in range(n)])]
where the time goes in v3:
time: 21.8 us; the launch traced here: 21.6 us
  starting transfers between devices  12.2 us (56%)
  waiting for transfers between devices  6.12 us (28%)
  Pallas kernels  3.22 us (15%)
    ppermute x9, starting transfers between devices, swap(): return lax.ppermute(v, axis, [(i, i ^ k) for i in range(n)])  12.2 us
    ppermute x9, waiting for transfers between devices, swap(): return lax.ppermute(v, axis, [(i, i ^ k) for i in range(n)])  6.12 us
    pallas_call x1, Pallas kernels, local(): pl.pallas_call(functools.partial(far_kernel, near_at, far_at), out_shape=...  1.32 us
    pallas_call x1, Pallas kernels, local(): pl.pallas_call(mask_kernel, out_shape=[pltpu.VMEM(a.shape, a.dtype), pltp...  1.29 us
    pallas_call x1, Pallas kernels, local(): pl.pallas_call(functools.partial(near_kernel, list(shards)), out_shape=[p...  0.6 us
  transfers between devices with their start and end apart: 9, of which 5 were waited for; matrix products, arithmetic and copies ran while one was open for 0% of the time, Pallas kernels for 3%

profile of v3, /device:TPU:0, one launch (start us, length us, event | category | flops | bytes accessed | tf_op | source)
XLA Modules:
  0.0 21.6 jit_solution(7304026203349812563)
XLA Ops:
  0.0 1.3 %shard_map.46 = (bf16[48,1024]{1,0:T(8,128)(2,1)S(1)}, bf16[1024,256]{1,0:T(8,128)(2,1)S(1)}) custom-call(s32[3,8]{1,0:T(4,128)} %amask.1, s32[2,8]{1,0:T(2,128)} %bitcast.1, bf16[48,1024]{1,0:T(8,128)(2,1)} %a.1, bf16[1024,256]{1,0:T(8,128)(2,1)} %b.1), custom_call_target="tpu_custom_call" | custom-call | tf_op jit(solution)/shard_map/pallas_call | solution.py:80
  1.3 3.0 %collective-permute-start.6 = (bf16[1024,256]{1,0:T(8,128)(2,1)S(1)}, bf16[1024,256]{1,0:T(8,128)(2,1)S(1)}, u32[]{:S(2)}, u32[]{:S(2)}) collective-permute-start(bf16[1024,256]{1,0:T(8,128)(2,1)S(1)} %get-tuple-element.31.refs_7_), channel_id=1, source_target_pairs={{0,16},{8,24},{16,0},{24,8},{1,17},{9,25},{17,1},{25,9},{2,18},{10... | collective-permute-start | bytes 1572872 | tf_op jit(solution)/shard_map/ppermute | solution.py:89
  4.3 2.6 %collective-permute-start.2 = (bf16[48,1024]{1,0:T(8,128)(2,1)S(1)}, bf16[48,1024]{1,0:T(8,128)(2,1)S(1)}, u32[]{:S(2)}, u32[]{:S(2)}) collective-permute-start(bf16[48,1024]{1,0:T(8,128)(2,1)S(1)} %get-tuple-element.19.refs_0_), channel_id=1, source_target_pairs={{0,4},{1,5},{2,6},{3,7},{4,0},{5,1},{6,2},{7,3},{8,12},{9,13},{10,... | collective-permute-start | bytes 294920 | tf_op jit(solution)/shard_map/ppermute | solution.py:89
  6.9 1.6 %collective-permute-start.1 = (bf16[48,1024]{1,0:T(8,128)(2,1)S(1)}, bf16[48,1024]{1,0:T(8,128)(2,1)S(1)}, u32[]{:S(2)}, u32[]{:S(2)}) collective-permute-start(bf16[48,1024]{1,0:T(8,128)(2,1)S(1)} %get-tuple-element.19.refs_0_), channel_id=1, source_target_pairs={{0,2},{1,3},{2,0},{3,1},{4,6},{5,7},{6,4},{7,5},{8,10},{9,11},{10,... | collective-permute-start | bytes 294920 | tf_op jit(solution)/shard_map/ppermute | solution.py:89
  8.5 1.5 %collective-permute-start = (bf16[48,1024]{1,0:T(8,128)(2,1)S(1)}, bf16[48,1024]{1,0:T(8,128)(2,1)S(1)}, u32[]{:S(2)}, u32[]{:S(2)}) collective-permute-start(bf16[48,1024]{1,0:T(8,128)(2,1)S(1)} %get-tuple-element.19.refs_0_), channel_id=1, source_target_pairs={{0,1},{1,0},{2,3},{3,2},{4,5},{5,4},{6,7},{7,6},{8,9},{9,8},{10,11... | collective-permute-start | bytes 294920 | tf_op jit(solution)/shard_map/ppermute | solution.py:89
  10.0 1.6 %collective-permute-done.2.refs_1_.refs_4_ = bf16[48,1024]{1,0:T(8,128)(2,1)S(1)} collective-permute-done((bf16[48,1024]{1,0:T(8,128)(2,1)S(1)}, bf16[48,1024]{1,0:T(8,128)(2,1)S(1)}, u32[]{:S(2)}, u32[]{:S(2)}) %collective-permute-start.2) | collective-permute-done | bytes 98336 | tf_op jit(solution)/shard_map/ppermute | solution.py:89
  11.6 0.4 %collective-permute-done.1.refs_0_.refs_2_ = bf16[48,1024]{1,0:T(8,128)(2,1)S(1)} collective-permute-done((bf16[48,1024]{1,0:T(8,128)(2,1)S(1)}, bf16[48,1024]{1,0:T(8,128)(2,1)S(1)}, u32[]{:S(2)}, u32[]{:S(2)}) %collective-permute-start.1) | collective-permute-done | bytes 98336 | tf_op jit(solution)/shard_map/ppermute | solution.py:89
  11.9 1.6 %collective-permute-start.4 = (bf16[96,1024]{1,0:T(8,128)(2,1)S(1)}, bf16[96,1024]{1,0:T(8,128)(2,1)S(1)}, u32[]{:S(2)}, u32[]{:S(2)}) collective-permute-start(bf16[96,1024]{1,0:T(8,128)(2,1)S(1)} %shard_map.47), channel_id=1, source_target_pairs={{0,1},{1,0},{2,3},{3,2},{4,5},{5,4},{6,7},{7,6},{8,9},{9,8},{10,11... | collective-permute-start | bytes 589832 | tf_op jit(solution)/shard_map/ppermute | solution.py:89
  13.5 1.5 %collective-permute-start.5 = (bf16[48,1024]{1,0:T(8,128)(2,1)S(1)}, bf16[48,1024]{1,0:T(8,128)(2,1)S(1)}, u32[]{:S(2)}, u32[]{:S(2)}) collective-permute-start(bf16[48,1024]{1,0:T(8,128)(2,1)S(1)} %collective-permute-done.2.refs_1_.refs_4_), channel_id=1, source_target_pairs={{0,3},{1,2},{2,1},{3,0},{4,7},{5,6},{6,5},{7,4},{8,11},{9,10},{10,... | collective-permute-start | bytes 294920 | tf_op jit(solution)/shard_map/ppermute | solution.py:89
  15.0 0.0 collective-permute-done.refs_1_
  15.0 0.5 %collective-permute-start.3 = (bf16[48,1024]{1,0:T(8,128)(2,1)S(1)}, bf16[48,1024]{1,0:T(8,128)(2,1)S(1)}, u32[]{:S(2)}, u32[]{:S(2)}) collective-permute-start(bf16[48,1024]{1,0:T(8,128)(2,1)S(1)} %collective-permute-done.2.refs_1_.refs_4_), channel_id=1, source_target_pairs={{0,2},{1,3},{2,0},{3,1},{4,6},{5,7},{6,4},{7,5},{8,10},{9,11},{10,... | collective-permute-start | bytes 294920 | tf_op jit(solution)/shard_map/ppermute | solution.py:89
  15.5 0.0 collective-permute-start.7
  15.5 0.7 %collective-permute-done.6.refs_8_ = bf16[1024,256]{1,0:T(8,128)(2,1)S(1)} collective-permute-done((bf16[1024,256]{1,0:T(8,128)(2,1)S(1)}, bf16[1024,256]{1,0:T(8,128)(2,1)S(1)}, u32[]{:S(2)}, u32[]{:S(2)}) %collective-permute-start.6) | collective-permute-done | bytes 524320 | tf_op jit(solution)/shard_map/ppermute | solution.py:89
  16.2 0.0 collective-permute-start.8
  16.2 3.0 %collective-permute-done.5.refs_6_ = bf16[48,1024]{1,0:T(8,128)(2,1)S(1)} collective-permute-done((bf16[48,1024]{1,0:T(8,128)(2,1)S(1)}, bf16[48,1024]{1,0:T(8,128)(2,1)S(1)}, u32[]{:S(2)}, u32[]{:S(2)}) %collective-permute-start.5) | collective-permute-done | bytes 98336 | tf_op jit(solution)/shard_map/ppermute | solution.py:89
  19.2 0.5 %collective-permute-done.4.refs_3_ = bf16[96,1024]{1,0:T(8,128)(2,1)S(1)} collective-permute-done((bf16[96,1024]{1,0:T(8,128)(2,1)S(1)}, bf16[96,1024]{1,0:T(8,128)(2,1)S(1)}, u32[]{:S(2)}, u32[]{:S(2)}) %collective-permute-start.4) | collective-permute-done | bytes 196640 | tf_op jit(solution)/shard_map/ppermute | solution.py:89
  19.7 0.0 collective-permute-done.3.refs_5_
  19.7 0.6 %shard_map.48 = (bf16[384,1024]{1,0:T(8,128)(2,1)S(1)}, bf16[2,384,256]{2,1,0:T(8,128)(2,1)S(1)}) custom-call(bf16[48,1024]{1,0:T(8,128)(2,1)S(1)} %get-tuple-element.19.refs_0_, bf16[48,1024]{1,0:T(8,128)(2,1)S(1)} %collective-permute-done.refs_1_, bf16[48,1024]{1,0:T(8,128)(2,1)S(1)} %collective-permute-done.1.refs_0_.refs_2_, ...), custom_call_target="tpu_custom_call" | custom-call | flops 5000000000 | bytes 4194304 | tf_op jit(solution)/shard_map/pallas_call | solution.py:135
  20.3 0.0 collective-permute-done.7.refs_0_
  20.3 0.0 collective-permute-done.8.refs_1_
  20.3 1.3 %shard_map.49 = bf16[384,1024]{1,0:T(8,128)(2,1)} custom-call(bf16[384,1024]{1,0:T(8,128)(2,1)S(1)} %get-tuple-element.29.a_all, bf16[2,384,256]{2,1,0:T(8,128)(2,1)S(1)} %get-tuple-element.30.near, bf16[1024,256]{1,0:T(8,128)(2,1)S(1)} %collective-permute-done.7.refs_0_, bf16[1024,256]{1,0:T(8,128)(2,1)S(1)} %collective-permute-done.8.refs_1_), custom_call_target="tpu_custom_call" | custom-call | tf_op jit(solution)/shard_map/pallas_call | solution.py:143
  (1 shorter events, 0.0 us)
Async XLA Ops:
  1.3 14.9 %collective-permute-start.6 = (bf16[1024,256]{1,0:T(8,128)(2,1)S(1)}, bf16[1024,256]{1,0:T(8,128)(2,1)S(1)}, u32[]{:S(2)}, u32[]{:S(2)}) collective-permute-start(bf16[1024,256]{1,0:T(8,128)(2,1)S(1)} %get-tuple-element.31.refs_7_), channel_id=1, source_target_pairs={{0,16},{8,24},{16,0},{24,8},{1,17},{9,25},{17,1},{25,9},{2,18},{10... | collective-permute-start | bytes 1572872 | tf_op jit(solution)/shard_map/ppermute | solution.py:89
  4.3 7.3 %collective-permute-start.2 = (bf16[48,1024]{1,0:T(8,128)(2,1)S(1)}, bf16[48,1024]{1,0:T(8,128)(2,1)S(1)}, u32[]{:S(2)}, u32[]{:S(2)}) collective-permute-start(bf16[48,1024]{1,0:T(8,128)(2,1)S(1)} %get-tuple-element.19.refs_0_), channel_id=1, source_target_pairs={{0,4},{1,5},{2,6},{3,7},{4,0},{5,1},{6,2},{7,3},{8,12},{9,13},{10,... | collective-permute-start | bytes 294920 | tf_op jit(solution)/shard_map/ppermute | solution.py:89
  6.9 5.0 %collective-permute-start.1 = (bf16[48,1024]{1,0:T(8,128)(2,1)S(1)}, bf16[48,1024]{1,0:T(8,128)(2,1)S(1)}, u32[]{:S(2)}, u32[]{:S(2)}) collective-permute-start(bf16[48,1024]{1,0:T(8,128)(2,1)S(1)} %get-tuple-element.19.refs_0_), channel_id=1, source_target_pairs={{0,2},{1,3},{2,0},{3,1},{4,6},{5,7},{6,4},{7,5},{8,10},{9,11},{10,... | collective-permute-start | bytes 294920 | tf_op jit(solution)/shard_map/ppermute | solution.py:89
  8.5 6.6 %collective-permute-start = (bf16[48,1024]{1,0:T(8,128)(2,1)S(1)}, bf16[48,1024]{1,0:T(8,128)(2,1)S(1)}, u32[]{:S(2)}, u32[]{:S(2)}) collective-permute-start(bf16[48,1024]{1,0:T(8,128)(2,1)S(1)} %get-tuple-element.19.refs_0_), channel_id=1, source_target_pairs={{0,1},{1,0},{2,3},{3,2},{4,5},{5,4},{6,7},{7,6},{8,9},{9,8},{10,11... | collective-permute-start | bytes 294920 | tf_op jit(solution)/shard_map/ppermute | solution.py:89
  11.9 7.7 %collective-permute-start.4 = (bf16[96,1024]{1,0:T(8,128)(2,1)S(1)}, bf16[96,1024]{1,0:T(8,128)(2,1)S(1)}, u32[]{:S(2)}, u32[]{:S(2)}) collective-permute-start(bf16[96,1024]{1,0:T(8,128)(2,1)S(1)} %shard_map.47), channel_id=1, source_target_pairs={{0,1},{1,0},{2,3},{3,2},{4,5},{5,4},{6,7},{7,6},{8,9},{9,8},{10,11... | collective-permute-start | bytes 589832 | tf_op jit(solution)/shard_map/ppermute | solution.py:89
  13.5 5.7 %collective-permute-start.5 = (bf16[48,1024]{1,0:T(8,128)(2,1)S(1)}, bf16[48,1024]{1,0:T(8,128)(2,1)S(1)}, u32[]{:S(2)}, u32[]{:S(2)}) collective-permute-start(bf16[48,1024]{1,0:T(8,128)(2,1)S(1)} %collective-permute-done.2.refs_1_.refs_4_), channel_id=1, source_target_pairs={{0,3},{1,2},{2,1},{3,0},{4,7},{5,6},{6,5},{7,4},{8,11},{9,10},{10,... | collective-permute-start | bytes 294920 | tf_op jit(solution)/shard_map/ppermute | solution.py:89
  15.0 4.6 %collective-permute-start.3 = (bf16[48,1024]{1,0:T(8,128)(2,1)S(1)}, bf16[48,1024]{1,0:T(8,128)(2,1)S(1)}, u32[]{:S(2)}, u32[]{:S(2)}) collective-permute-start(bf16[48,1024]{1,0:T(8,128)(2,1)S(1)} %collective-permute-done.2.refs_1_.refs_4_), channel_id=1, source_target_pairs={{0,2},{1,3},{2,0},{3,1},{4,6},{5,7},{6,4},{7,5},{8,10},{9,11},{10,... | collective-permute-start | bytes 294920 | tf_op jit(solution)/shard_map/ppermute | solution.py:89
  15.5 4.8 %collective-permute-start.7 = (bf16[1024,256]{1,0:T(8,128)(2,1)S(1)}, bf16[1024,256]{1,0:T(8,128)(2,1)S(1)}, u32[]{:S(2)}, u32[]{:S(2)}) collective-permute-start(bf16[1024,256]{1,0:T(8,128)(2,1)S(1)} %get-tuple-element.31.refs_7_), channel_id=1, source_target_pairs={{0,8},{8,0},{16,24},{24,16},{1,9},{9,1},{17,25},{25,17},{2,10},{10... | collective-permute-start | bytes 1572872 | tf_op jit(solution)/shard_map/ppermute | solution.py:89
  16.2 4.1 %collective-permute-start.8 = (bf16[1024,256]{1,0:T(8,128)(2,1)S(1)}, bf16[1024,256]{1,0:T(8,128)(2,1)S(1)}, u32[]{:S(2)}, u32[]{:S(2)}) collective-permute-start(bf16[1024,256]{1,0:T(8,128)(2,1)S(1)} %collective-permute-done.6.refs_8_), channel_id=1, source_target_pairs={{0,8},{8,0},{16,24},{24,16},{1,9},{9,1},{17,25},{25,17},{2,10},{10... | collective-permute-start | bytes 1572872 | tf_op jit(solution)/shard_map/ppermute | solution.py:89

commit v4 on v3

--- a/solution.py
+++ b/solution.py
@@ -44,34 +44,52 @@
     return (0.5 * jnp.dot(a, b, preferred_element_type=jnp.float32)).astype(dtype)
 
 
-def near_kernel(masks, *refs):
-    a_refs, b_refs, (a_all, near) = refs[: len(masks)], refs[len(masks) : -2], refs[-2:]
+def early_kernel(n_rows, *refs):
+    a_refs, b_refs, (early, a_early) = refs[:n_rows], refs[n_rows:-2], refs[-2:]
+    top = 0
+    for ref in a_refs:
+        a_early[top : top + ref.shape[0], :] = ref[...]
+        top += ref.shape[0]
+    for n, b in enumerate(b_refs):
+        early[n] = product(a_early[...], b[...], early.dtype)
+
+
+def rows_kernel(masks, late_at, *refs):
+    a_refs, (_, a_all, a_late) = refs[: len(masks)], refs[len(masks) :]
     for ks, ref in zip(masks, a_refs, strict=True):
         rows = ref.shape[0] // len(ks)
         for i, k in enumerate(ks):
             at = pl.multiple_of((lax.axis_index("grp") ^ k) * rows, OTILE)
             a_all[pl.ds(at, rows), :] = ref[i * rows : (i + 1) * rows, :]
-    for n, b in enumerate(b_refs):
-        near[n] = product(a_all[...], b[...], near.dtype)
+            if k in late_at:
+                top = late_at.index(k) * rows
+                a_late[top : top + rows, :] = ref[i * rows : (i + 1) * rows, :]
 
 
-def far_kernel(near_at, far_at, a_all, near, *refs):
-    b_refs, (out, stage, near_sems, far_sems) = refs[:-4], refs[-4:]
-    rows, width = near.shape[1:]
+def write_kernel(early_at, late_at, near_at, far_at, a_all, a_late, early, *refs):
+    b_refs, (out, stage, sems) = dict(zip(near_at + far_at, refs[:-3], strict=True)), refs[-3:]
+    tall, width = stage.shape[1:]
+    rows = tall // (len(early_at) + len(late_at))
+    copies = []
 
-    def write(block, k, top, sem):
-        at = pl.multiple_of((lax.axis_index("blk") ^ k) * width, TILE)
-        copy = pltpu.make_async_copy(block, out.at[pl.ds(top, block.shape[0]), pl.ds(at, width)], sem)
-        copy.start()
-        return copy
+    def write(k, top, height, sem):
+        col = pl.multiple_of((lax.axis_index("blk") ^ k) * width, TILE)
+        part = stage.at[k, top : top + height]
+        copies.append(pltpu.make_async_copy(part, out.at[top : top + height, pl.ds(col, width)], sem))
+        copies[-1].start()
 
-    copies = [write(near.at[n], k, 0, near_sems.at[n]) for n, k in enumerate(near_at)]
-    cuts = far_sems.shape[1]
-    for n, k in enumerate(far_at):
-        for c in range(cuts):
-            at = pl.ds(c * (rows // cuts), rows // cuts)
-            stage[n, at, :] = product(a_all[at, :], b_refs[n][...], stage.dtype)
-            copies.append(write(stage.at[n, at], k, c * (rows // cuts), far_sems.at[n, c]))
+    for n, k in enumerate(near_at):
+        late = product(a_late[...], b_refs[k][...], stage.dtype)
+        for at, found in ((early_at, early[n]), (late_at, late)):
+            for i, m in enumerate(at):
+                row = pl.multiple_of((lax.axis_index("grp") ^ m) * rows, OTILE)
+                stage[k, pl.ds(row, rows), :] = found[i * rows : (i + 1) * rows]
+        write(k, 0, tall, sems.at[k, 0])
+    for k in far_at:
+        for c in range(2):
+            top, height = c * (tall // 2), tall // 2
+            stage[k, top : top + height] = product(a_all[top : top + height], b_refs[k][...], stage.dtype)
+            write(k, top, height, sems.at[k, c])
     for copy in copies:
         copy.wait()
 
@@ -123,35 +141,47 @@
     m35 = along_grp(pair, 1)
     m7 = along_grp(z4, 3)
     m6 = along_grp(after(z4, z1), 2)
-    panels |= {k ^ 1: along_blk(after(v, z1), 1) for k, v in panels.items()}
+    first = {0: a_own, 1: z1, 2: z2, 4: z4}
+    rows, depth, width = a.shape[0] * n_grp, a.shape[1], b.shape[1]
+    out = jax.ShapeDtypeStruct((rows, width * n_blk), a.dtype)
+    near_at = tuple(range(0, n_blk, 2))
+    far_at = tuple(k for k in range(n_blk) if k not in near_at)
+    early_at = (0, 1, 2, 4)
+    late_at = tuple(k for k in range(n_grp) if k not in early_at)
+    tall = a.shape[0] * len(early_at)
+    soon = [first[k] for k in early_at] + [panels[k] for k in near_at]
+    early = pl.pallas_call(
+        functools.partial(early_kernel, len(early_at)),
+        out_shape=pltpu.VMEM((len(near_at), tall, width), a.dtype),
+        in_specs=[VMEM] * len(soon),
+        out_specs=VMEM,
+        scratch_shapes=[pltpu.VMEM((tall, depth), a.dtype)],
+        compiler_params=limit(out),
+        cost_estimate=pl.CostEstimate(flops=10**6, bytes_accessed=2**20, transcendentals=0),
+    )(*[held(v) for v in soon])
+    panels |= {k ^ 1: along_blk(after(v, z1, early) if k else after(v, z1), 1) for k, v in panels.items()}
     m7, m35, m6 = line(m7, m35, m6)
     shards = {(0,): a_own, (1,): z1, (2,): z2, (3, 5): m35, (4,): z4, (6,): m6, (7,): m7}
     for top in [8 << i for i in range((n_grp // 8).bit_length() - 1)]:
         shards[(top,)] = along_grp(a_own, top)
         shards |= {(top ^ k,): along_grp(shards[(top,)], k) for k in range(1, top)}
-    rows, depth, width = a.shape[0] * n_grp, a.shape[1], b.shape[1]
-    out = jax.ShapeDtypeStruct((rows, width * n_blk), a.dtype)
-    near_at, far_at = list(range(0, n_blk, 2)), list(range(1, n_blk, 2))
-    a_full, near = pl.pallas_call(
-        functools.partial(near_kernel, list(shards)),
-        out_shape=[pltpu.VMEM((rows, depth), a.dtype), pltpu.VMEM((len(near_at), rows, width), a.dtype)],
-        in_specs=[VMEM] * (len(shards) + len(near_at)),
+    a_all, a_late = pl.pallas_call(
+        functools.partial(rows_kernel, list(shards), late_at),
+        out_shape=[pltpu.VMEM((rows, depth), a.dtype), pltpu.VMEM((rows - tall, depth), a.dtype)],
+        in_specs=[VMEM] * (len(shards) + 1),
         out_specs=[VMEM, VMEM],
         compiler_params=limit(out),
-        cost_estimate=pl.CostEstimate(flops=50 * 10**8, bytes_accessed=2**22, transcendentals=0),
-    )(*[held(v) for v in [*shards.values()] + [panels[k] for k in near_at]])
+        cost_estimate=pl.CostEstimate(flops=52 * 10**8, bytes_accessed=2**22, transcendentals=0),
+    )(*[held(v) for v in [*shards.values(), early]])
+    ops = [a_all, a_late, early] + [panels[k] for k in near_at + far_at]
     return pl.pallas_call(
-        functools.partial(far_kernel, near_at, far_at),
+        functools.partial(write_kernel, early_at, late_at, near_at, far_at),
         out_shape=out,
-        in_specs=[VMEM] * (2 + len(far_at)),
+        in_specs=[VMEM] * len(ops),
         out_specs=ANY,
-        scratch_shapes=[
-            pltpu.VMEM((len(far_at), rows, width), a.dtype),
-            pltpu.SemaphoreType.DMA((len(near_at),)),
-            pltpu.SemaphoreType.DMA((len(far_at), 2)),
-        ],
+        scratch_shapes=[pltpu.VMEM((n_blk, rows, width), a.dtype), pltpu.SemaphoreType.DMA((n_blk, 2))],
         compiler_params=limit(out),
-    )(*[held(v) for v in [a_full, near] + [panels[k] for k in far_at]])
+    )(*[held(v) for v in ops])
 
 
 def solution(mesh):

time: 21.8 us -> 21.5 us (0.986)
  waiting for transfers between devices: 6.12 us -> 5.67 us
    ppermute x9, waiting for transfers between devices: 6.12 us -> 5.67 us  [swap(): return lax.ppermute(v, axis, [(i, i ^ k) for i in range(n)])]
    pallas_call x2 -> x3, Pallas kernels: 1.92 us -> 2 us  [the longest x1 1.54 us: local(): pl.pallas_call(functools.partial(write_kernel, early_at, late_at, near_at...]
  transfers between devices with their start and end apart: 9 -> 9, of which waited for: 5 -> 5; matrix products, arithmetic and copies ran while one was open for 0% -> 0% of each run, Pallas kernels for 3% -> 2%
where the time goes in v4:
time: 21.5 us; the launch traced here: 21.3 us
  starting transfers between devices  12.3 us (57%)
  waiting for transfers between devices  5.67 us (26%)
  Pallas kernels  3.3 us (15%)
    ppermute x9, starting transfers between devices, swap(): return lax.ppermute(v, axis, [(i, i ^ k) for i in range(n)])  12.3 us
    ppermute x9, waiting for transfers between devices, swap(): return lax.ppermute(v, axis, [(i, i ^ k) for i in range(n)])  5.67 us
    pallas_call x1, Pallas kernels, local(): pl.pallas_call(functools.partial(write_kernel, early_at, late_at, near_at...  1.54 us
    pallas_call x1, Pallas kernels, local(): pl.pallas_call(mask_kernel, out_shape=[pltpu.VMEM(a.shape, a.dtype), pltp...  1.29 us
  transfers between devices with their start and end apart: 9, of which 5 were waited for; matrix products, arithmetic and copies ran while one was open for 0% of the time, Pallas kernels for 2%

profile of v4, /device:TPU:0, one launch (start us, length us, event | category | flops | bytes accessed | tf_op | source)
XLA Modules:
  0.0 21.3 jit_solution(12156636416760501507)
XLA Ops:
  0.0 1.3 %shard_map.46 = (bf16[48,1024]{1,0:T(8,128)(2,1)S(1)}, bf16[1024,256]{1,0:T(8,128)(2,1)S(1)}) custom-call(s32[3,8]{1,0:T(4,128)} %amask.1, s32[2,8]{1,0:T(2,128)} %bitcast.1, bf16[48,1024]{1,0:T(8,128)(2,1)} %a.1, bf16[1024,256]{1,0:T(8,128)(2,1)} %b.1), custom_call_target="tpu_custom_call" | custom-call | tf_op jit(solution)/shard_map/pallas_call | solution.py:98
  1.3 3.0 %collective-permute-start.6 = (bf16[1024,256]{1,0:T(8,128)(2,1)S(1)}, bf16[1024,256]{1,0:T(8,128)(2,1)S(1)}, u32[]{:S(2)}, u32[]{:S(2)}) collective-permute-start(bf16[1024,256]{1,0:T(8,128)(2,1)S(1)} %get-tuple-element.31.refs_4_.refs_0_), channel_id=1, source_target_pairs={{0,16},{8,24},{16,0},{24,8},{1,17},{9,25},{17,1},{25,9},{2,18},{10... | collective-permute-start | bytes 1572872 | tf_op jit(solution)/shard_map/ppermute | solution.py:107
  4.3 2.6 %collective-permute-start.2 = (bf16[48,1024]{1,0:T(8,128)(2,1)S(1)}, bf16[48,1024]{1,0:T(8,128)(2,1)S(1)}, u32[]{:S(2)}, u32[]{:S(2)}) collective-permute-start(bf16[48,1024]{1,0:T(8,128)(2,1)S(1)} %get-tuple-element.19.refs_0_), channel_id=1, source_target_pairs={{0,4},{1,5},{2,6},{3,7},{4,0},{5,1},{6,2},{7,3},{8,12},{9,13},{10,... | collective-permute-start | bytes 294920 | tf_op jit(solution)/shard_map/ppermute | solution.py:107
  6.9 1.6 %collective-permute-start.1 = (bf16[48,1024]{1,0:T(8,128)(2,1)S(1)}, bf16[48,1024]{1,0:T(8,128)(2,1)S(1)}, u32[]{:S(2)}, u32[]{:S(2)}) collective-permute-start(bf16[48,1024]{1,0:T(8,128)(2,1)S(1)} %get-tuple-element.19.refs_0_), channel_id=1, source_target_pairs={{0,2},{1,3},{2,0},{3,1},{4,6},{5,7},{6,4},{7,5},{8,10},{9,11},{10,... | collective-permute-start | bytes 294920 | tf_op jit(solution)/shard_map/ppermute | solution.py:107
  8.5 1.5 %collective-permute-start = (bf16[48,1024]{1,0:T(8,128)(2,1)S(1)}, bf16[48,1024]{1,0:T(8,128)(2,1)S(1)}, u32[]{:S(2)}, u32[]{:S(2)}) collective-permute-start(bf16[48,1024]{1,0:T(8,128)(2,1)S(1)} %get-tuple-element.19.refs_0_), channel_id=1, source_target_pairs={{0,1},{1,0},{2,3},{3,2},{4,5},{5,4},{6,7},{7,6},{8,9},{9,8},{10,11... | collective-permute-start | bytes 294920 | tf_op jit(solution)/shard_map/ppermute | solution.py:107
  10.0 1.6 %collective-permute-done.2.refs_1_.refs_3_.refs_4_ = bf16[48,1024]{1,0:T(8,128)(2,1)S(1)} collective-permute-done((bf16[48,1024]{1,0:T(8,128)(2,1)S(1)}, bf16[48,1024]{1,0:T(8,128)(2,1)S(1)}, u32[]{:S(2)}, u32[]{:S(2)}) %collective-permute-start.2) | collective-permute-done | bytes 98336 | tf_op jit(solution)/shard_map/ppermute | solution.py:107
  11.6 0.4 %collective-permute-done.1.refs_0_.refs_2_ = bf16[48,1024]{1,0:T(8,128)(2,1)S(1)} collective-permute-done((bf16[48,1024]{1,0:T(8,128)(2,1)S(1)}, bf16[48,1024]{1,0:T(8,128)(2,1)S(1)}, u32[]{:S(2)}, u32[]{:S(2)}) %collective-permute-start.1) | collective-permute-done | bytes 98336 | tf_op jit(solution)/shard_map/ppermute | solution.py:107
  11.9 1.6 %collective-permute-start.4 = (bf16[96,1024]{1,0:T(8,128)(2,1)S(1)}, bf16[96,1024]{1,0:T(8,128)(2,1)S(1)}, u32[]{:S(2)}, u32[]{:S(2)}) collective-permute-start(bf16[96,1024]{1,0:T(8,128)(2,1)S(1)} %shard_map.47), channel_id=1, source_target_pairs={{0,1},{1,0},{2,3},{3,2},{4,5},{5,4},{6,7},{7,6},{8,9},{9,8},{10,11... | collective-permute-start | bytes 589832 | tf_op jit(solution)/shard_map/ppermute | solution.py:107
  13.5 1.5 %collective-permute-start.5 = (bf16[48,1024]{1,0:T(8,128)(2,1)S(1)}, bf16[48,1024]{1,0:T(8,128)(2,1)S(1)}, u32[]{:S(2)}, u32[]{:S(2)}) collective-permute-start(bf16[48,1024]{1,0:T(8,128)(2,1)S(1)} %collective-permute-done.2.refs_1_.refs_3_.refs_4_), channel_id=1, source_target_pairs={{0,3},{1,2},{2,1},{3,0},{4,7},{5,6},{6,5},{7,4},{8,11},{9,10},{10,... | collective-permute-start | bytes 294920 | tf_op jit(solution)/shard_map/ppermute | solution.py:107
  15.0 0.0 collective-permute-done.refs_1_
  15.0 0.5 %collective-permute-start.3 = (bf16[48,1024]{1,0:T(8,128)(2,1)S(1)}, bf16[48,1024]{1,0:T(8,128)(2,1)S(1)}, u32[]{:S(2)}, u32[]{:S(2)}) collective-permute-start(bf16[48,1024]{1,0:T(8,128)(2,1)S(1)} %collective-permute-done.2.refs_1_.refs_3_.refs_4_), channel_id=1, source_target_pairs={{0,2},{1,3},{2,0},{3,1},{4,6},{5,7},{6,4},{7,5},{8,10},{9,11},{10,... | collective-permute-start | bytes 294920 | tf_op jit(solution)/shard_map/ppermute | solution.py:107
  15.5 0.0 collective-permute-start.7
  15.5 0.7 %collective-permute-done.6.refs_5_.refs_1_ = bf16[1024,256]{1,0:T(8,128)(2,1)S(1)} collective-permute-done((bf16[1024,256]{1,0:T(8,128)(2,1)S(1)}, bf16[1024,256]{1,0:T(8,128)(2,1)S(1)}, u32[]{:S(2)}, u32[]{:S(2)}) %collective-permute-start.6) | collective-permute-done | bytes 524320 | tf_op jit(solution)/shard_map/ppermute | solution.py:107
  16.2 0.4 %shard_map.48.refs_7_.early = bf16[2,192,256]{2,1,0:T(8,128)(2,1)S(1)} custom-call(bf16[48,1024]{1,0:T(8,128)(2,1)S(1)} %get-tuple-element.19.refs_0_, bf16[48,1024]{1,0:T(8,128)(2,1)S(1)} %collective-permute-done.refs_1_, bf16[48,1024]{1,0:T(8,128)(2,1)S(1)} %collective-permute-done.1.refs_0_.refs_2_, ...), custom_call_target="tpu_custom_call" | custom-call | flops 1000000 | bytes 1048576 | tf_op jit(solution)/shard_map/pallas_call | solution.py:153
  16.6 0.1 collective-permute-start.8
  16.7 2.5 %collective-permute-done.5.refs_6_ = bf16[48,1024]{1,0:T(8,128)(2,1)S(1)} collective-permute-done((bf16[48,1024]{1,0:T(8,128)(2,1)S(1)}, bf16[48,1024]{1,0:T(8,128)(2,1)S(1)}, u32[]{:S(2)}, u32[]{:S(2)}) %collective-permute-start.5) | collective-permute-done | bytes 98336 | tf_op jit(solution)/shard_map/ppermute | solution.py:107
  19.2 0.5 %collective-permute-done.4.refs_3_ = bf16[96,1024]{1,0:T(8,128)(2,1)S(1)} collective-permute-done((bf16[96,1024]{1,0:T(8,128)(2,1)S(1)}, bf16[96,1024]{1,0:T(8,128)(2,1)S(1)}, u32[]{:S(2)}, u32[]{:S(2)}) %collective-permute-start.4) | collective-permute-done | bytes 196640 | tf_op jit(solution)/shard_map/ppermute | solution.py:107
  19.7 0.0 collective-permute-done.3.refs_5_
  19.7 0.1 shard_map.49
  19.8 0.0 collective-permute-done.7.refs_2_
  19.8 0.0 collective-permute-done.8.refs_3_
  19.8 1.5 %shard_map.50 = bf16[384,1024]{1,0:T(8,128)(2,1)} custom-call(bf16[384,1024]{1,0:T(8,128)(2,1)S(1)} %get-tuple-element.29.a_all, bf16[192,1024]{1,0:T(8,128)(2,1)S(1)} %get-tuple-element.30.a_late, bf16[2,192,256]{2,1,0:T(8,128)(2,1)S(1)} %shard_map.48.refs_7_.early, bf16[1024,256]{1,0:T(8,128)(2,1)S(1)} %get-tuple-element.31.refs_4_.refs_0_, ...), custom_call_target="tpu_custom_call" | custom-call | tf_op jit(solution)/shard_map/pallas_call | solution.py:177
  (1 shorter events, 0.0 us)
Async XLA Ops:
  1.3 14.9 %collective-permute-start.6 = (bf16[1024,256]{1,0:T(8,128)(2,1)S(1)}, bf16[1024,256]{1,0:T(8,128)(2,1)S(1)}, u32[]{:S(2)}, u32[]{:S(2)}) collective-permute-start(bf16[1024,256]{1,0:T(8,128)(2,1)S(1)} %get-tuple-element.31.refs_4_.refs_0_), channel_id=1, source_target_pairs={{0,16},{8,24},{16,0},{24,8},{1,17},{9,25},{17,1},{25,9},{2,18},{10... | collective-permute-start | bytes 1572872 | tf_op jit(solution)/shard_map/ppermute | solution.py:107
  4.3 7.3 %collective-permute-start.2 = (bf16[48,1024]{1,0:T(8,128)(2,1)S(1)}, bf16[48,1024]{1,0:T(8,128)(2,1)S(1)}, u32[]{:S(2)}, u32[]{:S(2)}) collective-permute-start(bf16[48,1024]{1,0:T(8,128)(2,1)S(1)} %get-tuple-element.19.refs_0_), channel_id=1, source_target_pairs={{0,4},{1,5},{2,6},{3,7},{4,0},{5,1},{6,2},{7,3},{8,12},{9,13},{10,... | collective-permute-start | bytes 294920 | tf_op jit(solution)/shard_map/ppermute | solution.py:107
  6.9 5.0 %collective-permute-start.1 = (bf16[48,1024]{1,0:T(8,128)(2,1)S(1)}, bf16[48,1024]{1,0:T(8,128)(2,1)S(1)}, u32[]{:S(2)}, u32[]{:S(2)}) collective-permute-start(bf16[48,1024]{1,0:T(8,128)(2,1)S(1)} %get-tuple-element.19.refs_0_), channel_id=1, source_target_pairs={{0,2},{1,3},{2,0},{3,1},{4,6},{5,7},{6,4},{7,5},{8,10},{9,11},{10,... | collective-permute-start | bytes 294920 | tf_op jit(solution)/shard_map/ppermute | solution.py:107
  8.5 6.6 %collective-permute-start = (bf16[48,1024]{1,0:T(8,128)(2,1)S(1)}, bf16[48,1024]{1,0:T(8,128)(2,1)S(1)}, u32[]{:S(2)}, u32[]{:S(2)}) collective-permute-start(bf16[48,1024]{1,0:T(8,128)(2,1)S(1)} %get-tuple-element.19.refs_0_), channel_id=1, source_target_pairs={{0,1},{1,0},{2,3},{3,2},{4,5},{5,4},{6,7},{7,6},{8,9},{9,8},{10,11... | collective-permute-start | bytes 294920 | tf_op jit(solution)/shard_map/ppermute | solution.py:107
  11.9 7.7 %collective-permute-start.4 = (bf16[96,1024]{1,0:T(8,128)(2,1)S(1)}, bf16[96,1024]{1,0:T(8,128)(2,1)S(1)}, u32[]{:S(2)}, u32[]{:S(2)}) collective-permute-start(bf16[96,1024]{1,0:T(8,128)(2,1)S(1)} %shard_map.47), channel_id=1, source_target_pairs={{0,1},{1,0},{2,3},{3,2},{4,5},{5,4},{6,7},{7,6},{8,9},{9,8},{10,11... | collective-permute-start | bytes 589832 | tf_op jit(solution)/shard_map/ppermute | solution.py:107
  13.5 5.7 %collective-permute-start.5 = (bf16[48,1024]{1,0:T(8,128)(2,1)S(1)}, bf16[48,1024]{1,0:T(8,128)(2,1)S(1)}, u32[]{:S(2)}, u32[]{:S(2)}) collective-permute-start(bf16[48,1024]{1,0:T(8,128)(2,1)S(1)} %collective-permute-done.2.refs_1_.refs_3_.refs_4_), channel_id=1, source_target_pairs={{0,3},{1,2},{2,1},{3,0},{4,7},{5,6},{6,5},{7,4},{8,11},{9,10},{10,... | collective-permute-start | bytes 294920 | tf_op jit(solution)/shard_map/ppermute | solution.py:107
  15.0 4.6 %collective-permute-start.3 = (bf16[48,1024]{1,0:T(8,128)(2,1)S(1)}, bf16[48,1024]{1,0:T(8,128)(2,1)S(1)}, u32[]{:S(2)}, u32[]{:S(2)}) collective-permute-start(bf16[48,1024]{1,0:T(8,128)(2,1)S(1)} %collective-permute-done.2.refs_1_.refs_3_.refs_4_), channel_id=1, source_target_pairs={{0,2},{1,3},{2,0},{3,1},{4,6},{5,7},{6,4},{7,5},{8,10},{9,11},{10,... | collective-permute-start | bytes 294920 | tf_op jit(solution)/shard_map/ppermute | solution.py:107
  15.5 4.3 %collective-permute-start.7 = (bf16[1024,256]{1,0:T(8,128)(2,1)S(1)}, bf16[1024,256]{1,0:T(8,128)(2,1)S(1)}, u32[]{:S(2)}, u32[]{:S(2)}) collective-permute-start(bf16[1024,256]{1,0:T(8,128)(2,1)S(1)} %get-tuple-element.31.refs_4_.refs_0_), channel_id=1, source_target_pairs={{0,8},{8,0},{16,24},{24,16},{1,9},{9,1},{17,25},{25,17},{2,10},{10... | collective-permute-start | bytes 1572872 | tf_op jit(solution)/shard_map/ppermute | solution.py:107
  16.6 3.2 %collective-permute-start.8 = (bf16[1024,256]{1,0:T(8,128)(2,1)S(1)}, bf16[1024,256]{1,0:T(8,128)(2,1)S(1)}, u32[]{:S(2)}, u32[]{:S(2)}) collective-permute-start(bf16[1024,256]{1,0:T(8,128)(2,1)S(1)} %collective-permute-done.6.refs_5_.refs_1_), channel_id=1, source_target_pairs={{0,8},{8,0},{16,24},{24,16},{1,9},{9,1},{17,25},{25,17},{2,10},{10... | collective-permute-start | bytes 1572872 | tf_op jit(solution)/shard_map/ppermute | solution.py:107

commit v5 on v4

--- a/solution.py
+++ b/solution.py
@@ -26,18 +26,30 @@
     return pltpu.with_memory_space_constraint(v, pltpu.VMEM)
 
 
-def mask_kernel(amask, bmask, a, b, a_out, b_out):
-    def factor(mask, i, j):
-        return mask[i, j].astype(jnp.float32).astype(a.dtype)
-
+def mask_kernel(amask, bmask, a, b, a_out, b_out, amask_here, bmask_here, a_here, b_here, sems):
+    depth = b.shape[0] // 2
+    pieces = [pl.ds(i * depth, depth) for i in range(2)]
+    moves = [(amask, amask_here), (bmask, bmask_here), (a, a_here)]
+    moves += [(b.at[piece], b_here.at[piece]) for piece in pieces]
+    copies = [pltpu.make_async_copy(*move, sems.at[i]) for i, move in enumerate(moves)]
+    for copy in copies:
+        copy.start()
+
+    def masked(v, mask, i, j):
+        return v * mask[i, j].astype(jnp.float32).astype(v.dtype)
+
+    for copy in copies[:3]:
+        copy.wait()
     for i in range(a.shape[0] // OTILE):
         for j in range(a.shape[1] // TILE):
             at = (slice(i * OTILE, (i + 1) * OTILE), slice(j * TILE, (j + 1) * TILE))
-            a_out[at] = a[at] * factor(amask, i, j)
+            a_out[at] = masked(a_here[at], amask_here, i, j)
     for i in range(b.shape[0] // TILE):
+        if i * TILE % depth == 0:
+            copies[3 + i * TILE // depth].wait()
         for j in range(b.shape[1] // TILE):
             at = (slice(i * TILE, (i + 1) * TILE), slice(j * TILE, (j + 1) * TILE))
-            b_out[at] = b[at] * factor(bmask, j, i)
+            b_out[at] = masked(b_here[at], bmask_here, j, i)
 
 
 def product(a, b, dtype):
@@ -98,8 +110,15 @@
     a_own, b_own = pl.pallas_call(
         mask_kernel,
         out_shape=[pltpu.VMEM(a.shape, a.dtype), pltpu.VMEM(b.shape, b.dtype)],
-        in_specs=[SMEM, SMEM, VMEM, VMEM],
+        in_specs=[ANY] * 4,
         out_specs=[VMEM, VMEM],
+        scratch_shapes=[
+            pltpu.SMEM(amask.shape, amask.dtype),
+            pltpu.SMEM(bmask.shape[::-1], bmask.dtype),
+            pltpu.VMEM(a.shape, a.dtype),
+            pltpu.VMEM(b.shape, b.dtype),
+            pltpu.SemaphoreType.DMA((2 + 3,)),
+        ],
         compiler_params=pltpu.CompilerParams(vmem_limit_bytes=56 * 2**20),
     )(amask, bmask.T, a, b)
 

time: 21.5 us -> 21.4 us (level)
  no operation moved by 1% of the time
where the time goes in v5:
time: 21.4 us; the launch traced here: 21.2 us
  starting transfers between devices  12.3 us (57%)
  waiting for transfers between devices  5.67 us (26%)
  Pallas kernels  3.19 us (15%)
    ppermute x9, starting transfers between devices, swap(): return lax.ppermute(v, axis, [(i, i ^ k) for i in range(n)])  12.3 us
    ppermute x9, waiting for transfers between devices, swap(): return lax.ppermute(v, axis, [(i, i ^ k) for i in range(n)])  5.67 us
    pallas_call x1, Pallas kernels, local(): pl.pallas_call(functools.partial(write_kernel, early_at, late_at, near_at...  1.54 us
    pallas_call x1, Pallas kernels, local(): pl.pallas_call(mask_kernel, out_shape=[pltpu.VMEM(a.shape, a.dtype), pltp...  1.18 us
  transfers between devices with their start and end apart: 9, of which 5 were waited for; matrix products, arithmetic and copies ran while one was open for 0% of the time, Pallas kernels for 2%

profile of v5, /device:TPU:0, one launch (start us, length us, event | category | flops | bytes accessed | tf_op | source)
XLA Modules:
  0.0 21.2 jit_solution(7965282182338445896)
XLA Ops:
  0.0 1.2 %shard_map.46 = (bf16[48,1024]{1,0:T(8,128)(2,1)S(1)}, bf16[1024,256]{1,0:T(8,128)(2,1)S(1)}) custom-call(s32[3,8]{1,0:T(4,128)} %amask.1, s32[2,8]{1,0:T(2,128)} %bitcast.1, bf16[48,1024]{1,0:T(8,128)(2,1)} %a.1, bf16[1024,256]{1,0:T(8,128)(2,1)} %b.1), custom_call_target="tpu_custom_call" | custom-call | tf_op jit(solution)/shard_map/pallas_call | solution.py:110
  1.2 3.0 %collective-permute-start.6 = (bf16[1024,256]{1,0:T(8,128)(2,1)S(1)}, bf16[1024,256]{1,0:T(8,128)(2,1)S(1)}, u32[]{:S(2)}, u32[]{:S(2)}) collective-permute-start(bf16[1024,256]{1,0:T(8,128)(2,1)S(1)} %get-tuple-element.31.refs_4_.refs_0_), channel_id=1, source_target_pairs={{0,16},{8,24},{16,0},{24,8},{1,17},{9,25},{17,1},{25,9},{2,18},{10... | collective-permute-start | bytes 1572872 | tf_op jit(solution)/shard_map/ppermute | solution.py:126
  4.2 2.6 %collective-permute-start.2 = (bf16[48,1024]{1,0:T(8,128)(2,1)S(1)}, bf16[48,1024]{1,0:T(8,128)(2,1)S(1)}, u32[]{:S(2)}, u32[]{:S(2)}) collective-permute-start(bf16[48,1024]{1,0:T(8,128)(2,1)S(1)} %get-tuple-element.19.refs_0_), channel_id=1, source_target_pairs={{0,4},{1,5},{2,6},{3,7},{4,0},{5,1},{6,2},{7,3},{8,12},{9,13},{10,... | collective-permute-start | bytes 294920 | tf_op jit(solution)/shard_map/ppermute | solution.py:126
  6.8 1.6 %collective-permute-start.1 = (bf16[48,1024]{1,0:T(8,128)(2,1)S(1)}, bf16[48,1024]{1,0:T(8,128)(2,1)S(1)}, u32[]{:S(2)}, u32[]{:S(2)}) collective-permute-start(bf16[48,1024]{1,0:T(8,128)(2,1)S(1)} %get-tuple-element.19.refs_0_), channel_id=1, source_target_pairs={{0,2},{1,3},{2,0},{3,1},{4,6},{5,7},{6,4},{7,5},{8,10},{9,11},{10,... | collective-permute-start | bytes 294920 | tf_op jit(solution)/shard_map/ppermute | solution.py:126
  8.4 1.5 %collective-permute-start = (bf16[48,1024]{1,0:T(8,128)(2,1)S(1)}, bf16[48,1024]{1,0:T(8,128)(2,1)S(1)}, u32[]{:S(2)}, u32[]{:S(2)}) collective-permute-start(bf16[48,1024]{1,0:T(8,128)(2,1)S(1)} %get-tuple-element.19.refs_0_), channel_id=1, source_target_pairs={{0,1},{1,0},{2,3},{3,2},{4,5},{5,4},{6,7},{7,6},{8,9},{9,8},{10,11... | collective-permute-start | bytes 294920 | tf_op jit(solution)/shard_map/ppermute | solution.py:126
  9.9 1.6 %collective-permute-done.2.refs_1_.refs_3_.refs_4_ = bf16[48,1024]{1,0:T(8,128)(2,1)S(1)} collective-permute-done((bf16[48,1024]{1,0:T(8,128)(2,1)S(1)}, bf16[48,1024]{1,0:T(8,128)(2,1)S(1)}, u32[]{:S(2)}, u32[]{:S(2)}) %collective-permute-start.2) | collective-permute-done | bytes 98336 | tf_op jit(solution)/shard_map/ppermute | solution.py:126
  11.5 0.4 %collective-permute-done.1.refs_0_.refs_2_ = bf16[48,1024]{1,0:T(8,128)(2,1)S(1)} collective-permute-done((bf16[48,1024]{1,0:T(8,128)(2,1)S(1)}, bf16[48,1024]{1,0:T(8,128)(2,1)S(1)}, u32[]{:S(2)}, u32[]{:S(2)}) %collective-permute-start.1) | collective-permute-done | bytes 98336 | tf_op jit(solution)/shard_map/ppermute | solution.py:126
  11.8 1.6 %collective-permute-start.4 = (bf16[96,1024]{1,0:T(8,128)(2,1)S(1)}, bf16[96,1024]{1,0:T(8,128)(2,1)S(1)}, u32[]{:S(2)}, u32[]{:S(2)}) collective-permute-start(bf16[96,1024]{1,0:T(8,128)(2,1)S(1)} %shard_map.47), channel_id=1, source_target_pairs={{0,1},{1,0},{2,3},{3,2},{4,5},{5,4},{6,7},{7,6},{8,9},{9,8},{10,11... | collective-permute-start | bytes 589832 | tf_op jit(solution)/shard_map/ppermute | solution.py:126
  13.4 1.5 %collective-permute-start.5 = (bf16[48,1024]{1,0:T(8,128)(2,1)S(1)}, bf16[48,1024]{1,0:T(8,128)(2,1)S(1)}, u32[]{:S(2)}, u32[]{:S(2)}) collective-permute-start(bf16[48,1024]{1,0:T(8,128)(2,1)S(1)} %collective-permute-done.2.refs_1_.refs_3_.refs_4_), channel_id=1, source_target_pairs={{0,3},{1,2},{2,1},{3,0},{4,7},{5,6},{6,5},{7,4},{8,11},{9,10},{10,... | collective-permute-start | bytes 294920 | tf_op jit(solution)/shard_map/ppermute | solution.py:126
  14.9 0.0 collective-permute-done.refs_1_
  14.9 0.5 %collective-permute-start.3 = (bf16[48,1024]{1,0:T(8,128)(2,1)S(1)}, bf16[48,1024]{1,0:T(8,128)(2,1)S(1)}, u32[]{:S(2)}, u32[]{:S(2)}) collective-permute-start(bf16[48,1024]{1,0:T(8,128)(2,1)S(1)} %collective-permute-done.2.refs_1_.refs_3_.refs_4_), channel_id=1, source_target_pairs={{0,2},{1,3},{2,0},{3,1},{4,6},{5,7},{6,4},{7,5},{8,10},{9,11},{10,... | collective-permute-start | bytes 294920 | tf_op jit(solution)/shard_map/ppermute | solution.py:126
  15.4 0.0 collective-permute-start.7
  15.4 0.7 %collective-permute-done.6.refs_5_.refs_1_ = bf16[1024,256]{1,0:T(8,128)(2,1)S(1)} collective-permute-done((bf16[1024,256]{1,0:T(8,128)(2,1)S(1)}, bf16[1024,256]{1,0:T(8,128)(2,1)S(1)}, u32[]{:S(2)}, u32[]{:S(2)}) %collective-permute-start.6) | collective-permute-done | bytes 524320 | tf_op jit(solution)/shard_map/ppermute | solution.py:126
  16.1 0.4 %shard_map.48.refs_7_.early = bf16[2,192,256]{2,1,0:T(8,128)(2,1)S(1)} custom-call(bf16[48,1024]{1,0:T(8,128)(2,1)S(1)} %get-tuple-element.19.refs_0_, bf16[48,1024]{1,0:T(8,128)(2,1)S(1)} %collective-permute-done.refs_1_, bf16[48,1024]{1,0:T(8,128)(2,1)S(1)} %collective-permute-done.1.refs_0_.refs_2_, ...), custom_call_target="tpu_custom_call" | custom-call | flops 1000000 | bytes 1048576 | tf_op jit(solution)/shard_map/pallas_call | solution.py:172
  16.5 0.1 collective-permute-start.8
  16.6 2.5 %collective-permute-done.5.refs_6_ = bf16[48,1024]{1,0:T(8,128)(2,1)S(1)} collective-permute-done((bf16[48,1024]{1,0:T(8,128)(2,1)S(1)}, bf16[48,1024]{1,0:T(8,128)(2,1)S(1)}, u32[]{:S(2)}, u32[]{:S(2)}) %collective-permute-start.5) | collective-permute-done | bytes 98336 | tf_op jit(solution)/shard_map/ppermute | solution.py:126
  19.1 0.5 %collective-permute-done.4.refs_3_ = bf16[96,1024]{1,0:T(8,128)(2,1)S(1)} collective-permute-done((bf16[96,1024]{1,0:T(8,128)(2,1)S(1)}, bf16[96,1024]{1,0:T(8,128)(2,1)S(1)}, u32[]{:S(2)}, u32[]{:S(2)}) %collective-permute-start.4) | collective-permute-done | bytes 196640 | tf_op jit(solution)/shard_map/ppermute | solution.py:126
  19.6 0.0 collective-permute-done.3.refs_5_
  19.6 0.1 shard_map.49
  19.7 0.0 collective-permute-done.7.refs_2_
  19.7 0.0 collective-permute-done.8.refs_3_
  19.7 1.5 %shard_map.50 = bf16[384,1024]{1,0:T(8,128)(2,1)} custom-call(bf16[384,1024]{1,0:T(8,128)(2,1)S(1)} %get-tuple-element.29.a_all, bf16[192,1024]{1,0:T(8,128)(2,1)S(1)} %get-tuple-element.30.a_late, bf16[2,192,256]{2,1,0:T(8,128)(2,1)S(1)} %shard_map.48.refs_7_.early, bf16[1024,256]{1,0:T(8,128)(2,1)S(1)} %get-tuple-element.31.refs_4_.refs_0_, ...), custom_call_target="tpu_custom_call" | custom-call | tf_op jit(solution)/shard_map/pallas_call | solution.py:196
  (1 shorter events, 0.0 us)
Async XLA Ops:
  1.2 14.9 %collective-permute-start.6 = (bf16[1024,256]{1,0:T(8,128)(2,1)S(1)}, bf16[1024,256]{1,0:T(8,128)(2,1)S(1)}, u32[]{:S(2)}, u32[]{:S(2)}) collective-permute-start(bf16[1024,256]{1,0:T(8,128)(2,1)S(1)} %get-tuple-element.31.refs_4_.refs_0_), channel_id=1, source_target_pairs={{0,16},{8,24},{16,0},{24,8},{1,17},{9,25},{17,1},{25,9},{2,18},{10... | collective-permute-start | bytes 1572872 | tf_op jit(solution)/shard_map/ppermute | solution.py:126
  4.2 7.3 %collective-permute-start.2 = (bf16[48,1024]{1,0:T(8,128)(2,1)S(1)}, bf16[48,1024]{1,0:T(8,128)(2,1)S(1)}, u32[]{:S(2)}, u32[]{:S(2)}) collective-permute-start(bf16[48,1024]{1,0:T(8,128)(2,1)S(1)} %get-tuple-element.19.refs_0_), channel_id=1, source_target_pairs={{0,4},{1,5},{2,6},{3,7},{4,0},{5,1},{6,2},{7,3},{8,12},{9,13},{10,... | collective-permute-start | bytes 294920 | tf_op jit(solution)/shard_map/ppermute | solution.py:126
  6.8 5.0 %collective-permute-start.1 = (bf16[48,1024]{1,0:T(8,128)(2,1)S(1)}, bf16[48,1024]{1,0:T(8,128)(2,1)S(1)}, u32[]{:S(2)}, u32[]{:S(2)}) collective-permute-start(bf16[48,1024]{1,0:T(8,128)(2,1)S(1)} %get-tuple-element.19.refs_0_), channel_id=1, source_target_pairs={{0,2},{1,3},{2,0},{3,1},{4,6},{5,7},{6,4},{7,5},{8,10},{9,11},{10,... | collective-permute-start | bytes 294920 | tf_op jit(solution)/shard_map/ppermute | solution.py:126
  8.4 6.6 %collective-permute-start = (bf16[48,1024]{1,0:T(8,128)(2,1)S(1)}, bf16[48,1024]{1,0:T(8,128)(2,1)S(1)}, u32[]{:S(2)}, u32[]{:S(2)}) collective-permute-start(bf16[48,1024]{1,0:T(8,128)(2,1)S(1)} %get-tuple-element.19.refs_0_), channel_id=1, source_target_pairs={{0,1},{1,0},{2,3},{3,2},{4,5},{5,4},{6,7},{7,6},{8,9},{9,8},{10,11... | collective-permute-start | bytes 294920 | tf_op jit(solution)/shard_map/ppermute | solution.py:126
  11.8 7.7 %collective-permute-start.4 = (bf16[96,1024]{1,0:T(8,128)(2,1)S(1)}, bf16[96,1024]{1,0:T(8,128)(2,1)S(1)}, u32[]{:S(2)}, u32[]{:S(2)}) collective-permute-start(bf16[96,1024]{1,0:T(8,128)(2,1)S(1)} %shard_map.47), channel_id=1, source_target_pairs={{0,1},{1,0},{2,3},{3,2},{4,5},{5,4},{6,7},{7,6},{8,9},{9,8},{10,11... | collective-permute-start | bytes 589832 | tf_op jit(solution)/shard_map/ppermute | solution.py:126
  13.4 5.7 %collective-permute-start.5 = (bf16[48,1024]{1,0:T(8,128)(2,1)S(1)}, bf16[48,1024]{1,0:T(8,128)(2,1)S(1)}, u32[]{:S(2)}, u32[]{:S(2)}) collective-permute-start(bf16[48,1024]{1,0:T(8,128)(2,1)S(1)} %collective-permute-done.2.refs_1_.refs_3_.refs_4_), channel_id=1, source_target_pairs={{0,3},{1,2},{2,1},{3,0},{4,7},{5,6},{6,5},{7,4},{8,11},{9,10},{10,... | collective-permute-start | bytes 294920 | tf_op jit(solution)/shard_map/ppermute | solution.py:126
  14.9 4.6 %collective-permute-start.3 = (bf16[48,1024]{1,0:T(8,128)(2,1)S(1)}, bf16[48,1024]{1,0:T(8,128)(2,1)S(1)}, u32[]{:S(2)}, u32[]{:S(2)}) collective-permute-start(bf16[48,1024]{1,0:T(8,128)(2,1)S(1)} %collective-permute-done.2.refs_1_.refs_3_.refs_4_), channel_id=1, source_target_pairs={{0,2},{1,3},{2,0},{3,1},{4,6},{5,7},{6,4},{7,5},{8,10},{9,11},{10,... | collective-permute-start | bytes 294920 | tf_op jit(solution)/shard_map/ppermute | solution.py:126
  15.4 4.3 %collective-permute-start.7 = (bf16[1024,256]{1,0:T(8,128)(2,1)S(1)}, bf16[1024,256]{1,0:T(8,128)(2,1)S(1)}, u32[]{:S(2)}, u32[]{:S(2)}) collective-permute-start(bf16[1024,256]{1,0:T(8,128)(2,1)S(1)} %get-tuple-element.31.refs_4_.refs_0_), channel_id=1, source_target_pairs={{0,8},{8,0},{16,24},{24,16},{1,9},{9,1},{17,25},{25,17},{2,10},{10... | collective-permute-start | bytes 1572872 | tf_op jit(solution)/shard_map/ppermute | solution.py:126
  16.5 3.2 %collective-permute-start.8 = (bf16[1024,256]{1,0:T(8,128)(2,1)S(1)}, bf16[1024,256]{1,0:T(8,128)(2,1)S(1)}, u32[]{:S(2)}, u32[]{:S(2)}) collective-permute-start(bf16[1024,256]{1,0:T(8,128)(2,1)S(1)} %collective-permute-done.6.refs_5_.refs_1_), channel_id=1, source_target_pairs={{0,8},{8,0},{16,24},{24,16},{1,9},{9,1},{17,25},{25,17},{2,10},{10... | collective-permute-start | bytes 1572872 | tf_op jit(solution)/shard_map/ppermute | solution.py:126

commit v6 on v5

--- a/solution.py
+++ b/solution.py
@@ -78,7 +78,7 @@
                 a_late[top : top + rows, :] = ref[i * rows : (i + 1) * rows, :]
 
 
-def write_kernel(early_at, late_at, near_at, far_at, a_all, a_late, early, *refs):
+def write_kernel(early_at, late_at, near_at, far_at, a_all, a_late, early_own, early, *refs):
     b_refs, (out, stage, sems) = dict(zip(near_at + far_at, refs[:-3], strict=True)), refs[-3:]
     tall, width = stage.shape[1:]
     rows = tall // (len(early_at) + len(late_at))
@@ -91,8 +91,9 @@
         copies[-1].start()
 
     for n, k in enumerate(near_at):
+        begun = early[n - 1] if n else early_own[0]
         late = product(a_late[...], b_refs[k][...], stage.dtype)
-        for at, found in ((early_at, early[n]), (late_at, late)):
+        for at, found in ((early_at, begun), (late_at, late)):
             for i, m in enumerate(at):
                 row = pl.multiple_of((lax.axis_index("grp") ^ m) * rows, OTILE)
                 stage[k, pl.ds(row, rows), :] = found[i * rows : (i + 1) * rows]
@@ -168,16 +169,21 @@
     early_at = (0, 1, 2, 4)
     late_at = tuple(k for k in range(n_grp) if k not in early_at)
     tall = a.shape[0] * len(early_at)
-    soon = [first[k] for k in early_at] + [panels[k] for k in near_at]
-    early = pl.pallas_call(
-        functools.partial(early_kernel, len(early_at)),
-        out_shape=pltpu.VMEM((len(near_at), tall, width), a.dtype),
-        in_specs=[VMEM] * len(soon),
-        out_specs=VMEM,
-        scratch_shapes=[pltpu.VMEM((tall, depth), a.dtype)],
-        compiler_params=limit(out),
-        cost_estimate=pl.CostEstimate(flops=10**6, bytes_accessed=2**20, transcendentals=0),
-    )(*[held(v) for v in soon])
+    soon = [first[k] for k in early_at]
+
+    def begun(at):
+        ops = soon + [panels[k] for k in at]
+        return pl.pallas_call(
+            functools.partial(early_kernel, len(soon)),
+            out_shape=pltpu.VMEM((len(at), tall, width), a.dtype),
+            in_specs=[VMEM] * len(ops),
+            out_specs=VMEM,
+            scratch_shapes=[pltpu.VMEM((tall, depth), a.dtype)],
+            compiler_params=limit(out),
+            cost_estimate=pl.CostEstimate(flops=10**6, bytes_accessed=2**20, transcendentals=0),
+        )(*[held(v) for v in ops])
+
+    early_own, early = begun(near_at[:1]), begun(near_at[1:])
     panels |= {k ^ 1: along_blk(after(v, z1, early) if k else after(v, z1), 1) for k, v in panels.items()}
     m7, m35, m6 = line(m7, m35, m6)
     shards = {(0,): a_own, (1,): z1, (2,): z2, (3, 5): m35, (4,): z4, (6,): m6, (7,): m7}
@@ -192,7 +198,7 @@
         compiler_params=limit(out),
         cost_estimate=pl.CostEstimate(flops=52 * 10**8, bytes_accessed=2**22, transcendentals=0),
     )(*[held(v) for v in [*shards.values(), early]])
-    ops = [a_all, a_late, early] + [panels[k] for k in near_at + far_at]
+    ops = [a_all, a_late, early_own, early] + [panels[k] for k in near_at + far_at]
     return pl.pallas_call(
         functools.partial(write_kernel, early_at, late_at, near_at, far_at),
         out_shape=out,

time: 21.4 us -> 21.4 us (level)
    pallas_call x1 -> x2, Pallas kernels: 0.37 us -> 0.54 us  [begun(): pl.pallas_call(functools.partial(early_kernel, len(soon)), out_shape=pltp...]
  transfers between devices with their start and end apart: 9 -> 9, of which waited for: 5 -> 5; matrix products, arithmetic and copies ran while one was open for 0% -> 0% of each run, Pallas kernels for 2% -> 3%
where the time goes in v6:
time: 21.4 us; the launch traced here: 21.2 us
  starting transfers between devices  12.3 us (57%)
  waiting for transfers between devices  5.5 us (26%)
  Pallas kernels  3.36 us (16%)
    ppermute x9, starting transfers between devices, swap(): return lax.ppermute(v, axis, [(i, i ^ k) for i in range(n)])  12.3 us
    ppermute x9, waiting for transfers between devices, swap(): return lax.ppermute(v, axis, [(i, i ^ k) for i in range(n)])  5.5 us
    pallas_call x1, Pallas kernels, local(): pl.pallas_call(functools.partial(write_kernel, early_at, late_at, near_at...  1.54 us
    pallas_call x1, Pallas kernels, local(): pl.pallas_call(mask_kernel, out_shape=[pltpu.VMEM(a.shape, a.dtype), pltp...  1.18 us
    pallas_call x2, Pallas kernels, begun(): pl.pallas_call(functools.partial(early_kernel, len(soon)), out_shape=pltp...  0.54 us
  transfers between devices with their start and end apart: 9, of which 5 were waited for; matrix products, arithmetic and copies ran while one was open for 0% of the time, Pallas kernels for 3%

profile of v6, /device:TPU:0, one launch (start us, length us, event | category | flops | bytes accessed | tf_op | source)
XLA Modules:
  0.0 21.2 jit_solution(2962364355198142124)
XLA Ops:
  0.0 1.2 %shard_map.46 = (bf16[48,1024]{1,0:T(8,128)(2,1)S(1)}, bf16[1024,256]{1,0:T(8,128)(2,1)S(1)}) custom-call(s32[3,8]{1,0:T(4,128)} %amask.1, s32[2,8]{1,0:T(2,128)} %bitcast.1, bf16[48,1024]{1,0:T(8,128)(2,1)} %a.1, bf16[1024,256]{1,0:T(8,128)(2,1)} %b.1), custom_call_target="tpu_custom_call" | custom-call | tf_op jit(solution)/shard_map/pallas_call | solution.py:111
  1.2 3.0 %collective-permute-start.6 = (bf16[1024,256]{1,0:T(8,128)(2,1)S(1)}, bf16[1024,256]{1,0:T(8,128)(2,1)S(1)}, u32[]{:S(2)}, u32[]{:S(2)}) collective-permute-start(bf16[1024,256]{1,0:T(8,128)(2,1)S(1)} %get-tuple-element.31.refs_4_.refs_0_), channel_id=1, source_target_pairs={{0,16},{8,24},{16,0},{24,8},{1,17},{9,25},{17,1},{25,9},{2,18},{10... | collective-permute-start | bytes 1572872 | tf_op jit(solution)/shard_map/ppermute | solution.py:127
  4.2 2.6 %collective-permute-start.2 = (bf16[48,1024]{1,0:T(8,128)(2,1)S(1)}, bf16[48,1024]{1,0:T(8,128)(2,1)S(1)}, u32[]{:S(2)}, u32[]{:S(2)}) collective-permute-start(bf16[48,1024]{1,0:T(8,128)(2,1)S(1)} %get-tuple-element.19.refs_0_), channel_id=1, source_target_pairs={{0,4},{1,5},{2,6},{3,7},{4,0},{5,1},{6,2},{7,3},{8,12},{9,13},{10,... | collective-permute-start | bytes 294920 | tf_op jit(solution)/shard_map/ppermute | solution.py:127
  6.8 1.6 %collective-permute-start.1 = (bf16[48,1024]{1,0:T(8,128)(2,1)S(1)}, bf16[48,1024]{1,0:T(8,128)(2,1)S(1)}, u32[]{:S(2)}, u32[]{:S(2)}) collective-permute-start(bf16[48,1024]{1,0:T(8,128)(2,1)S(1)} %get-tuple-element.19.refs_0_), channel_id=1, source_target_pairs={{0,2},{1,3},{2,0},{3,1},{4,6},{5,7},{6,4},{7,5},{8,10},{9,11},{10,... | collective-permute-start | bytes 294920 | tf_op jit(solution)/shard_map/ppermute | solution.py:127
  8.4 1.5 %collective-permute-start = (bf16[48,1024]{1,0:T(8,128)(2,1)S(1)}, bf16[48,1024]{1,0:T(8,128)(2,1)S(1)}, u32[]{:S(2)}, u32[]{:S(2)}) collective-permute-start(bf16[48,1024]{1,0:T(8,128)(2,1)S(1)} %get-tuple-element.19.refs_0_), channel_id=1, source_target_pairs={{0,1},{1,0},{2,3},{3,2},{4,5},{5,4},{6,7},{7,6},{8,9},{9,8},{10,11... | collective-permute-start | bytes 294920 | tf_op jit(solution)/shard_map/ppermute | solution.py:127
  9.9 1.6 %collective-permute-done.2.refs_1_.refs_3_.refs_4_ = bf16[48,1024]{1,0:T(8,128)(2,1)S(1)} collective-permute-done((bf16[48,1024]{1,0:T(8,128)(2,1)S(1)}, bf16[48,1024]{1,0:T(8,128)(2,1)S(1)}, u32[]{:S(2)}, u32[]{:S(2)}) %collective-permute-start.2) | collective-permute-done | bytes 98336 | tf_op jit(solution)/shard_map/ppermute | solution.py:127
  11.5 0.4 %collective-permute-done.1.refs_0_.refs_2_ = bf16[48,1024]{1,0:T(8,128)(2,1)S(1)} collective-permute-done((bf16[48,1024]{1,0:T(8,128)(2,1)S(1)}, bf16[48,1024]{1,0:T(8,128)(2,1)S(1)}, u32[]{:S(2)}, u32[]{:S(2)}) %collective-permute-start.1) | collective-permute-done | bytes 98336 | tf_op jit(solution)/shard_map/ppermute | solution.py:127
  11.8 1.6 %collective-permute-start.4 = (bf16[96,1024]{1,0:T(8,128)(2,1)S(1)}, bf16[96,1024]{1,0:T(8,128)(2,1)S(1)}, u32[]{:S(2)}, u32[]{:S(2)}) collective-permute-start(bf16[96,1024]{1,0:T(8,128)(2,1)S(1)} %shard_map.47), channel_id=1, source_target_pairs={{0,1},{1,0},{2,3},{3,2},{4,5},{5,4},{6,7},{7,6},{8,9},{9,8},{10,11... | collective-permute-start | bytes 589832 | tf_op jit(solution)/shard_map/ppermute | solution.py:127
  13.4 1.5 %collective-permute-start.5 = (bf16[48,1024]{1,0:T(8,128)(2,1)S(1)}, bf16[48,1024]{1,0:T(8,128)(2,1)S(1)}, u32[]{:S(2)}, u32[]{:S(2)}) collective-permute-start(bf16[48,1024]{1,0:T(8,128)(2,1)S(1)} %collective-permute-done.2.refs_1_.refs_3_.refs_4_), channel_id=1, source_target_pairs={{0,3},{1,2},{2,1},{3,0},{4,7},{5,6},{6,5},{7,4},{8,11},{9,10},{10,... | collective-permute-start | bytes 294920 | tf_op jit(solution)/shard_map/ppermute | solution.py:127
  14.9 0.0 collective-permute-done.refs_1_
  14.9 0.5 %collective-permute-start.3 = (bf16[48,1024]{1,0:T(8,128)(2,1)S(1)}, bf16[48,1024]{1,0:T(8,128)(2,1)S(1)}, u32[]{:S(2)}, u32[]{:S(2)}) collective-permute-start(bf16[48,1024]{1,0:T(8,128)(2,1)S(1)} %collective-permute-done.2.refs_1_.refs_3_.refs_4_), channel_id=1, source_target_pairs={{0,2},{1,3},{2,0},{3,1},{4,6},{5,7},{6,4},{7,5},{8,10},{9,11},{10,... | collective-permute-start | bytes 294920 | tf_op jit(solution)/shard_map/ppermute | solution.py:127
  15.4 0.0 collective-permute-start.7
  15.4 0.7 %collective-permute-done.6.refs_4_.refs_1_ = bf16[1024,256]{1,0:T(8,128)(2,1)S(1)} collective-permute-done((bf16[1024,256]{1,0:T(8,128)(2,1)S(1)}, bf16[1024,256]{1,0:T(8,128)(2,1)S(1)}, u32[]{:S(2)}, u32[]{:S(2)}) %collective-permute-start.6) | collective-permute-done | bytes 524320 | tf_op jit(solution)/shard_map/ppermute | solution.py:127
  16.1 0.3 %shard_map.48.refs_7_.early = bf16[1,192,256]{2,1,0:T(8,128)(2,1)S(1)} custom-call(bf16[48,1024]{1,0:T(8,128)(2,1)S(1)} %get-tuple-element.19.refs_0_, bf16[48,1024]{1,0:T(8,128)(2,1)S(1)} %collective-permute-done.refs_1_, bf16[48,1024]{1,0:T(8,128)(2,1)S(1)} %collective-permute-done.1.refs_0_.refs_2_, ...), custom_call_target="tpu_custom_call" | custom-call | flops 1000000 | bytes 1048576 | tf_op jit(solution)/shard_map/pallas_call | solution.py:176
  16.4 0.1 collective-permute-start.8
  16.5 0.3 %shard_map.50.early_own = bf16[1,192,256]{2,1,0:T(8,128)(2,1)S(1)} custom-call(bf16[48,1024]{1,0:T(8,128)(2,1)S(1)} %get-tuple-element.19.refs_0_, bf16[48,1024]{1,0:T(8,128)(2,1)S(1)} %collective-permute-done.refs_1_, bf16[48,1024]{1,0:T(8,128)(2,1)S(1)} %collective-permute-done.1.refs_0_.refs_2_, ...), custom_call_target="tpu_custom_call" | custom-call | flops 1000000 | bytes 1048576 | tf_op jit(solution)/shard_map/pallas_call | solution.py:176
  16.7 2.3 %collective-permute-done.5.refs_6_ = bf16[48,1024]{1,0:T(8,128)(2,1)S(1)} collective-permute-done((bf16[48,1024]{1,0:T(8,128)(2,1)S(1)}, bf16[48,1024]{1,0:T(8,128)(2,1)S(1)}, u32[]{:S(2)}, u32[]{:S(2)}) %collective-permute-start.5) | collective-permute-done | bytes 98336 | tf_op jit(solution)/shard_map/ppermute | solution.py:127
  19.1 0.5 %collective-permute-done.4.refs_3_ = bf16[96,1024]{1,0:T(8,128)(2,1)S(1)} collective-permute-done((bf16[96,1024]{1,0:T(8,128)(2,1)S(1)}, bf16[96,1024]{1,0:T(8,128)(2,1)S(1)}, u32[]{:S(2)}, u32[]{:S(2)}) %collective-permute-start.4) | collective-permute-done | bytes 196640 | tf_op jit(solution)/shard_map/ppermute | solution.py:127
  19.6 0.0 collective-permute-done.3.refs_5_
  19.6 0.1 shard_map.49
  19.7 0.0 collective-permute-done.7.refs_2_
  19.7 0.0 collective-permute-done.8.refs_3_
  19.7 1.5 %shard_map.51 = bf16[384,1024]{1,0:T(8,128)(2,1)} custom-call(bf16[384,1024]{1,0:T(8,128)(2,1)S(1)} %get-tuple-element.29.a_all, bf16[192,1024]{1,0:T(8,128)(2,1)S(1)} %get-tuple-element.30.a_late, bf16[1,192,256]{2,1,0:T(8,128)(2,1)S(1)} %shard_map.50.early_own, bf16[1,192,256]{2,1,0:T(8,128)(2,1)S(1)} %shard_map.48.refs_7_.early, ...), custom_call_target="tpu_custom_call" | custom-call | tf_op jit(solution)/shard_map/pallas_call | solution.py:202
  (1 shorter events, 0.0 us)
Async XLA Ops:
  1.2 14.9 %collective-permute-start.6 = (bf16[1024,256]{1,0:T(8,128)(2,1)S(1)}, bf16[1024,256]{1,0:T(8,128)(2,1)S(1)}, u32[]{:S(2)}, u32[]{:S(2)}) collective-permute-start(bf16[1024,256]{1,0:T(8,128)(2,1)S(1)} %get-tuple-element.31.refs_4_.refs_0_), channel_id=1, source_target_pairs={{0,16},{8,24},{16,0},{24,8},{1,17},{9,25},{17,1},{25,9},{2,18},{10... | collective-permute-start | bytes 1572872 | tf_op jit(solution)/shard_map/ppermute | solution.py:127
  4.2 7.3 %collective-permute-start.2 = (bf16[48,1024]{1,0:T(8,128)(2,1)S(1)}, bf16[48,1024]{1,0:T(8,128)(2,1)S(1)}, u32[]{:S(2)}, u32[]{:S(2)}) collective-permute-start(bf16[48,1024]{1,0:T(8,128)(2,1)S(1)} %get-tuple-element.19.refs_0_), channel_id=1, source_target_pairs={{0,4},{1,5},{2,6},{3,7},{4,0},{5,1},{6,2},{7,3},{8,12},{9,13},{10,... | collective-permute-start | bytes 294920 | tf_op jit(solution)/shard_map/ppermute | solution.py:127
  6.8 5.0 %collective-permute-start.1 = (bf16[48,1024]{1,0:T(8,128)(2,1)S(1)}, bf16[48,1024]{1,0:T(8,128)(2,1)S(1)}, u32[]{:S(2)}, u32[]{:S(2)}) collective-permute-start(bf16[48,1024]{1,0:T(8,128)(2,1)S(1)} %get-tuple-element.19.refs_0_), channel_id=1, source_target_pairs={{0,2},{1,3},{2,0},{3,1},{4,6},{5,7},{6,4},{7,5},{8,10},{9,11},{10,... | collective-permute-start | bytes 294920 | tf_op jit(solution)/shard_map/ppermute | solution.py:127
  8.4 6.6 %collective-permute-start = (bf16[48,1024]{1,0:T(8,128)(2,1)S(1)}, bf16[48,1024]{1,0:T(8,128)(2,1)S(1)}, u32[]{:S(2)}, u32[]{:S(2)}) collective-permute-start(bf16[48,1024]{1,0:T(8,128)(2,1)S(1)} %get-tuple-element.19.refs_0_), channel_id=1, source_target_pairs={{0,1},{1,0},{2,3},{3,2},{4,5},{5,4},{6,7},{7,6},{8,9},{9,8},{10,11... | collective-permute-start | bytes 294920 | tf_op jit(solution)/shard_map/ppermute | solution.py:127
  11.8 7.7 %collective-permute-start.4 = (bf16[96,1024]{1,0:T(8,128)(2,1)S(1)}, bf16[96,1024]{1,0:T(8,128)(2,1)S(1)}, u32[]{:S(2)}, u32[]{:S(2)}) collective-permute-start(bf16[96,1024]{1,0:T(8,128)(2,1)S(1)} %shard_map.47), channel_id=1, source_target_pairs={{0,1},{1,0},{2,3},{3,2},{4,5},{5,4},{6,7},{7,6},{8,9},{9,8},{10,11... | collective-permute-start | bytes 589832 | tf_op jit(solution)/shard_map/ppermute | solution.py:127
  13.4 5.7 %collective-permute-start.5 = (bf16[48,1024]{1,0:T(8,128)(2,1)S(1)}, bf16[48,1024]{1,0:T(8,128)(2,1)S(1)}, u32[]{:S(2)}, u32[]{:S(2)}) collective-permute-start(bf16[48,1024]{1,0:T(8,128)(2,1)S(1)} %collective-permute-done.2.refs_1_.refs_3_.refs_4_), channel_id=1, source_target_pairs={{0,3},{1,2},{2,1},{3,0},{4,7},{5,6},{6,5},{7,4},{8,11},{9,10},{10,... | collective-permute-start | bytes 294920 | tf_op jit(solution)/shard_map/ppermute | solution.py:127
  14.9 4.6 %collective-permute-start.3 = (bf16[48,1024]{1,0:T(8,128)(2,1)S(1)}, bf16[48,1024]{1,0:T(8,128)(2,1)S(1)}, u32[]{:S(2)}, u32[]{:S(2)}) collective-permute-start(bf16[48,1024]{1,0:T(8,128)(2,1)S(1)} %collective-permute-done.2.refs_1_.refs_3_.refs_4_), channel_id=1, source_target_pairs={{0,2},{1,3},{2,0},{3,1},{4,6},{5,7},{6,4},{7,5},{8,10},{9,11},{10,... | collective-permute-start | bytes 294920 | tf_op jit(solution)/shard_map/ppermute | solution.py:127
  15.4 4.3 %collective-permute-start.7 = (bf16[1024,256]{1,0:T(8,128)(2,1)S(1)}, bf16[1024,256]{1,0:T(8,128)(2,1)S(1)}, u32[]{:S(2)}, u32[]{:S(2)}) collective-permute-start(bf16[1024,256]{1,0:T(8,128)(2,1)S(1)} %get-tuple-element.31.refs_4_.refs_0_), channel_id=1, source_target_pairs={{0,8},{8,0},{16,24},{24,16},{1,9},{9,1},{17,25},{25,17},{2,10},{10... | collective-permute-start | bytes 1572872 | tf_op jit(solution)/shard_map/ppermute | solution.py:127
  16.4 3.3 %collective-permute-start.8 = (bf16[1024,256]{1,0:T(8,128)(2,1)S(1)}, bf16[1024,256]{1,0:T(8,128)(2,1)S(1)}, u32[]{:S(2)}, u32[]{:S(2)}) collective-permute-start(bf16[1024,256]{1,0:T(8,128)(2,1)S(1)} %collective-permute-done.6.refs_4_.refs_1_), channel_id=1, source_target_pairs={{0,8},{8,0},{16,24},{24,16},{1,9},{9,1},{17,25},{25,17},{2,10},{10... | collective-permute-start | bytes 1572872 | tf_op jit(solution)/shard_map/ppermute | solution.py:127

commit v7 on v5

--- a/solution.py
+++ b/solution.py
@@ -125,7 +125,7 @@
     def swap(v, axis, n, k):
         return lax.ppermute(v, axis, [(i, i ^ k) for i in range(n)])
 
-    def joined(*vs):
+    def joined(*vs, flops=10**6):
         def join_kernel(*refs):
             top = 0
             for ref in refs[:-1]:
@@ -139,6 +139,7 @@
             in_specs=[VMEM] * len(vs),
             out_specs=VMEM,
             compiler_params=limit(*vs),
+            cost_estimate=pl.CostEstimate(flops=flops, bytes_accessed=2**18, transcendentals=0),
         )(*[held(v) for v in vs])
 
     def line(*vs):
@@ -154,23 +155,20 @@
         return swap(v, "blk", n_blk, k)
 
     panels = {0: b_own} | {k: along_blk(b_own, k) for k in range(2, n_blk, 2)}
-    z4, z2, z1 = along_grp(a_own, 4), along_grp(a_own, 2), along_grp(a_own, 1)
-    z4, z2 = line(z4, z2)
-    pair = joined(z2, z4)
-    m35 = along_grp(pair, 1)
-    m7 = along_grp(z4, 3)
-    m6 = along_grp(after(z4, z1), 2)
-    first = {0: a_own, 1: z1, 2: z2, 4: z4}
+    z4, z1 = along_grp(a_own, 4), along_grp(a_own, 1)
+    a2 = along_grp(joined(a_own, z1), 2)
+    z4_on = joined(z4, flops=12 * 10**8)
+    m7, m5, m6 = along_grp(z4_on, 3), along_grp(z4_on, 1), along_grp(z4_on, 2)
     rows, depth, width = a.shape[0] * n_grp, a.shape[1], b.shape[1]
     out = jax.ShapeDtypeStruct((rows, width * n_blk), a.dtype)
     near_at = tuple(range(0, n_blk, 2))
     far_at = tuple(k for k in range(n_blk) if k not in near_at)
-    early_at = (0, 1, 2, 4)
+    early_at = (0, 1, 2, 3, 4)
     late_at = tuple(k for k in range(n_grp) if k not in early_at)
     tall = a.shape[0] * len(early_at)
-    soon = [first[k] for k in early_at] + [panels[k] for k in near_at]
+    soon = [a_own, z1, a2, z4] + [panels[k] for k in near_at]
     early = pl.pallas_call(
-        functools.partial(early_kernel, len(early_at)),
+        functools.partial(early_kernel, 4),
         out_shape=pltpu.VMEM((len(near_at), tall, width), a.dtype),
         in_specs=[VMEM] * len(soon),
         out_specs=VMEM,
@@ -178,9 +176,9 @@
         compiler_params=limit(out),
         cost_estimate=pl.CostEstimate(flops=10**6, bytes_accessed=2**20, transcendentals=0),
     )(*[held(v) for v in soon])
-    panels |= {k ^ 1: along_blk(after(v, z1, early) if k else after(v, z1), 1) for k, v in panels.items()}
-    m7, m35, m6 = line(m7, m35, m6)
-    shards = {(0,): a_own, (1,): z1, (2,): z2, (3, 5): m35, (4,): z4, (6,): m6, (7,): m7}
+    panels |= {k ^ 1: along_blk(after(v, early) if k else after(v, a2), 1) for k, v in panels.items()}
+    a2, m7, m5, m6 = line(a2, m7, m5, m6)
+    shards = {(0,): a_own, (1,): z1, (2, 3): a2, (4,): z4, (5,): m5, (6,): m6, (7,): m7}
     for top in [8 << i for i in range((n_grp // 8).bit_length() - 1)]:
         shards[(top,)] = along_grp(a_own, top)
         shards |= {(top ^ k,): along_grp(shards[(top,)], k) for k in range(1, top)}

time: 21.4 us -> 21.4 us (level)
  starting transfers between devices: 12.3 us -> 12.9 us
  waiting for transfers between devices: 5.67 us -> 5.14 us
    ppermute x9, starting transfers between devices: 12.3 us -> 12.9 us  [swap(): return lax.ppermute(v, axis, [(i, i ^ k) for i in range(n)])]
    ppermute x9, waiting for transfers between devices: 5.67 us -> 5.14 us  [swap(): return lax.ppermute(v, axis, [(i, i ^ k) for i in range(n)])]
where the time goes in v7:
time: 21.4 us; the launch traced here: 21.3 us
  starting transfers between devices  12.9 us (60%)
  waiting for transfers between devices  5.14 us (24%)
  Pallas kernels  3.19 us (15%)
    ppermute x9, starting transfers between devices, swap(): return lax.ppermute(v, axis, [(i, i ^ k) for i in range(n)])  12.9 us
    ppermute x9, waiting for transfers between devices, swap(): return lax.ppermute(v, axis, [(i, i ^ k) for i in range(n)])  5.14 us
    pallas_call x1, Pallas kernels, local(): pl.pallas_call(functools.partial(write_kernel, early_at, late_at, near_at...  1.48 us
    pallas_call x1, Pallas kernels, local(): pl.pallas_call(mask_kernel, out_shape=[pltpu.VMEM(a.shape, a.dtype), pltp...  1.18 us
  transfers between devices with their start and end apart: 9, of which 5 were waited for; matrix products, arithmetic and copies ran while one was open for 0% of the time, Pallas kernels for 2%

profile of v7, /device:TPU:0, one launch (start us, length us, event | category | flops | bytes accessed | tf_op | source)
XLA Modules:
  0.0 21.3 jit_solution(2792819987604896498)
XLA Ops:
  0.0 1.2 %shard_map.46 = (bf16[48,1024]{1,0:T(8,128)(2,1)S(1)}, bf16[1024,256]{1,0:T(8,128)(2,1)S(1)}) custom-call(s32[3,8]{1,0:T(4,128)} %amask.1, s32[2,8]{1,0:T(2,128)} %bitcast.1, bf16[48,1024]{1,0:T(8,128)(2,1)} %a.1, bf16[1024,256]{1,0:T(8,128)(2,1)} %b.1), custom_call_target="tpu_custom_call" | custom-call | tf_op jit(solution)/shard_map/pallas_call | solution.py:110
  1.2 3.0 %collective-permute-start.6 = (bf16[1024,256]{1,0:T(8,128)(2,1)S(1)}, bf16[1024,256]{1,0:T(8,128)(2,1)S(1)}, u32[]{:S(2)}, u32[]{:S(2)}) collective-permute-start(bf16[1024,256]{1,0:T(8,128)(2,1)S(1)} %get-tuple-element.33.refs_4_.refs_0_), channel_id=1, source_target_pairs={{0,16},{8,24},{16,0},{24,8},{1,17},{9,25},{17,1},{25,9},{2,18},{10... | collective-permute-start | bytes 1572872 | tf_op jit(solution)/shard_map/ppermute | solution.py:126
  4.2 1.5 %collective-permute-start = (bf16[48,1024]{1,0:T(8,128)(2,1)S(1)}, bf16[48,1024]{1,0:T(8,128)(2,1)S(1)}, u32[]{:S(2)}, u32[]{:S(2)}) collective-permute-start(bf16[48,1024]{1,0:T(8,128)(2,1)S(1)} %get-tuple-element.20.refs_0_), channel_id=1, source_target_pairs={{0,1},{1,0},{2,3},{3,2},{4,5},{5,4},{6,7},{7,6},{8,9},{9,8},{10,11... | collective-permute-start | bytes 294920 | tf_op jit(solution)/shard_map/ppermute | solution.py:126
  5.7 2.6 %collective-permute-start.1 = (bf16[48,1024]{1,0:T(8,128)(2,1)S(1)}, bf16[48,1024]{1,0:T(8,128)(2,1)S(1)}, u32[]{:S(2)}, u32[]{:S(2)}) collective-permute-start(bf16[48,1024]{1,0:T(8,128)(2,1)S(1)} %get-tuple-element.20.refs_0_), channel_id=1, source_target_pairs={{0,4},{1,5},{2,6},{3,7},{4,0},{5,1},{6,2},{7,3},{8,12},{9,13},{10,... | collective-permute-start | bytes 294920 | tf_op jit(solution)/shard_map/ppermute | solution.py:126
  8.3 0.5 %collective-permute-done.refs_1_ = bf16[48,1024]{1,0:T(8,128)(2,1)S(1)} collective-permute-done((bf16[48,1024]{1,0:T(8,128)(2,1)S(1)}, bf16[48,1024]{1,0:T(8,128)(2,1)S(1)}, u32[]{:S(2)}, u32[]{:S(2)}) %collective-permute-start) | collective-permute-done | bytes 98336 | tf_op jit(solution)/shard_map/ppermute | solution.py:126
  8.8 1.6 %collective-permute-start.5 = (bf16[96,1024]{1,0:T(8,128)(2,1)S(1)}, bf16[96,1024]{1,0:T(8,128)(2,1)S(1)}, u32[]{:S(2)}, u32[]{:S(2)}) collective-permute-start(bf16[96,1024]{1,0:T(8,128)(2,1)S(1)} %shard_map.48), channel_id=1, source_target_pairs={{0,2},{1,3},{2,0},{3,1},{4,6},{5,7},{6,4},{7,5},{8,10},{9,11},{10,... | collective-permute-start | bytes 589832 | tf_op jit(solution)/shard_map/ppermute | solution.py:126
  10.5 2.3 %collective-permute-done.1.refs_0_.refs_3_ = bf16[48,1024]{1,0:T(8,128)(2,1)S(1)} collective-permute-done((bf16[48,1024]{1,0:T(8,128)(2,1)S(1)}, bf16[48,1024]{1,0:T(8,128)(2,1)S(1)}, u32[]{:S(2)}, u32[]{:S(2)}) %collective-permute-start.1) | collective-permute-done | bytes 98336 | tf_op jit(solution)/shard_map/ppermute | solution.py:126
  12.8 0.6 %collective-permute-start.4 = (bf16[48,1024]{1,0:T(8,128)(2,1)S(1)}, bf16[48,1024]{1,0:T(8,128)(2,1)S(1)}, u32[]{:S(2)}, u32[]{:S(2)}) collective-permute-start(bf16[48,1024]{1,0:T(8,128)(2,1)S(1)} %shard_map.47), channel_id=1, source_target_pairs={{0,3},{1,2},{2,1},{3,0},{4,7},{5,6},{6,5},{7,4},{8,11},{9,10},{10,... | collective-permute-start | bytes 294920 | tf_op jit(solution)/shard_map/ppermute | solution.py:126
  13.4 1.5 %collective-permute-start.3 = (bf16[48,1024]{1,0:T(8,128)(2,1)S(1)}, bf16[48,1024]{1,0:T(8,128)(2,1)S(1)}, u32[]{:S(2)}, u32[]{:S(2)}) collective-permute-start(bf16[48,1024]{1,0:T(8,128)(2,1)S(1)} %shard_map.47), channel_id=1, source_target_pairs={{0,1},{1,0},{2,3},{3,2},{4,5},{5,4},{6,7},{7,6},{8,9},{9,8},{10,11... | collective-permute-start | bytes 294920 | tf_op jit(solution)/shard_map/ppermute | solution.py:126
  14.9 1.5 %collective-permute-start.2 = (bf16[48,1024]{1,0:T(8,128)(2,1)S(1)}, bf16[48,1024]{1,0:T(8,128)(2,1)S(1)}, u32[]{:S(2)}, u32[]{:S(2)}) collective-permute-start(bf16[48,1024]{1,0:T(8,128)(2,1)S(1)} %shard_map.47), channel_id=1, source_target_pairs={{0,2},{1,3},{2,0},{3,1},{4,6},{5,7},{6,4},{7,5},{8,10},{9,11},{10,... | collective-permute-start | bytes 294920 | tf_op jit(solution)/shard_map/ppermute | solution.py:126
  16.4 0.7 %collective-permute-done.5.refs_2_ = bf16[96,1024]{1,0:T(8,128)(2,1)S(1)} collective-permute-done((bf16[96,1024]{1,0:T(8,128)(2,1)S(1)}, bf16[96,1024]{1,0:T(8,128)(2,1)S(1)}, u32[]{:S(2)}, u32[]{:S(2)}) %collective-permute-start.5) | collective-permute-done | bytes 196640 | tf_op jit(solution)/shard_map/ppermute | solution.py:126
  17.1 0.0 collective-permute-start.7
  17.1 0.0 collective-permute-done.6.refs_5_.refs_1_
  17.1 0.4 %shard_map.49.refs_7_.early = bf16[2,240,256]{2,1,0:T(8,128)(2,1)S(1)} custom-call(bf16[48,1024]{1,0:T(8,128)(2,1)S(1)} %get-tuple-element.20.refs_0_, bf16[48,1024]{1,0:T(8,128)(2,1)S(1)} %collective-permute-done.refs_1_, bf16[96,1024]{1,0:T(8,128)(2,1)S(1)} %collective-permute-done.5.refs_2_, bf16[48,1024]{1,0:T(8,128)(2,1)S(1)} %collective-permute-done.1.refs_0_.refs_3_, ...), custom_call_target="tpu_custom_call" | custom-call | flops 1000000 | bytes 1048576 | tf_op jit(solution)/shard_map/pallas_call | solution.py:170
  17.5 0.6 %collective-permute-start.8 = (bf16[1024,256]{1,0:T(8,128)(2,1)S(1)}, bf16[1024,256]{1,0:T(8,128)(2,1)S(1)}, u32[]{:S(2)}, u32[]{:S(2)}) collective-permute-start(bf16[1024,256]{1,0:T(8,128)(2,1)S(1)} %collective-permute-done.6.refs_5_.refs_1_), channel_id=1, source_target_pairs={{0,8},{8,0},{16,24},{24,16},{1,9},{9,1},{17,25},{25,17},{2,10},{10... | collective-permute-start | bytes 1572872 | tf_op jit(solution)/shard_map/ppermute | solution.py:126
  18.1 1.0 %collective-permute-done.4.refs_6_ = bf16[48,1024]{1,0:T(8,128)(2,1)S(1)} collective-permute-done((bf16[48,1024]{1,0:T(8,128)(2,1)S(1)}, bf16[48,1024]{1,0:T(8,128)(2,1)S(1)}, u32[]{:S(2)}, u32[]{:S(2)}) %collective-permute-start.4) | collective-permute-done | bytes 98336 | tf_op jit(solution)/shard_map/ppermute | solution.py:126
  19.0 0.0 collective-permute-done.3.refs_4_
  19.0 0.6 %collective-permute-done.2.refs_5_ = bf16[48,1024]{1,0:T(8,128)(2,1)S(1)} collective-permute-done((bf16[48,1024]{1,0:T(8,128)(2,1)S(1)}, bf16[48,1024]{1,0:T(8,128)(2,1)S(1)}, u32[]{:S(2)}, u32[]{:S(2)}) %collective-permute-start.2) | collective-permute-done | bytes 98336 | tf_op jit(solution)/shard_map/ppermute | solution.py:126
  19.7 0.1 shard_map.50
  19.8 0.0 collective-permute-done.7.refs_2_
  19.8 0.0 collective-permute-done.8.refs_3_
  19.8 1.5 %shard_map.51 = bf16[384,1024]{1,0:T(8,128)(2,1)} custom-call(bf16[384,1024]{1,0:T(8,128)(2,1)S(1)} %get-tuple-element.31.a_all, bf16[144,1024]{1,0:T(8,128)(2,1)S(1)} %get-tuple-element.32.a_late, bf16[2,240,256]{2,1,0:T(8,128)(2,1)S(1)} %shard_map.49.refs_7_.early, bf16[1024,256]{1,0:T(8,128)(2,1)S(1)} %get-tuple-element.33.refs_4_.refs_0_, ...), custom_call_target="tpu_custom_call" | custom-call | tf_op jit(solution)/shard_map/pallas_call | solution.py:194
  (2 shorter events, 0.0 us)
Async XLA Ops:
  1.2 15.9 %collective-permute-start.6 = (bf16[1024,256]{1,0:T(8,128)(2,1)S(1)}, bf16[1024,256]{1,0:T(8,128)(2,1)S(1)}, u32[]{:S(2)}, u32[]{:S(2)}) collective-permute-start(bf16[1024,256]{1,0:T(8,128)(2,1)S(1)} %get-tuple-element.33.refs_4_.refs_0_), channel_id=1, source_target_pairs={{0,16},{8,24},{16,0},{24,8},{1,17},{9,25},{17,1},{25,9},{2,18},{10... | collective-permute-start | bytes 1572872 | tf_op jit(solution)/shard_map/ppermute | solution.py:126
  4.2 4.6 %collective-permute-start = (bf16[48,1024]{1,0:T(8,128)(2,1)S(1)}, bf16[48,1024]{1,0:T(8,128)(2,1)S(1)}, u32[]{:S(2)}, u32[]{:S(2)}) collective-permute-start(bf16[48,1024]{1,0:T(8,128)(2,1)S(1)} %get-tuple-element.20.refs_0_), channel_id=1, source_target_pairs={{0,1},{1,0},{2,3},{3,2},{4,5},{5,4},{6,7},{7,6},{8,9},{9,8},{10,11... | collective-permute-start | bytes 294920 | tf_op jit(solution)/shard_map/ppermute | solution.py:126
  5.7 7.1 %collective-permute-start.1 = (bf16[48,1024]{1,0:T(8,128)(2,1)S(1)}, bf16[48,1024]{1,0:T(8,128)(2,1)S(1)}, u32[]{:S(2)}, u32[]{:S(2)}) collective-permute-start(bf16[48,1024]{1,0:T(8,128)(2,1)S(1)} %get-tuple-element.20.refs_0_), channel_id=1, source_target_pairs={{0,4},{1,5},{2,6},{3,7},{4,0},{5,1},{6,2},{7,3},{8,12},{9,13},{10,... | collective-permute-start | bytes 294920 | tf_op jit(solution)/shard_map/ppermute | solution.py:126
  8.8 8.2 %collective-permute-start.5 = (bf16[96,1024]{1,0:T(8,128)(2,1)S(1)}, bf16[96,1024]{1,0:T(8,128)(2,1)S(1)}, u32[]{:S(2)}, u32[]{:S(2)}) collective-permute-start(bf16[96,1024]{1,0:T(8,128)(2,1)S(1)} %shard_map.48), channel_id=1, source_target_pairs={{0,2},{1,3},{2,0},{3,1},{4,6},{5,7},{6,4},{7,5},{8,10},{9,11},{10,... | collective-permute-start | bytes 589832 | tf_op jit(solution)/shard_map/ppermute | solution.py:126
  12.8 6.2 %collective-permute-start.4 = (bf16[48,1024]{1,0:T(8,128)(2,1)S(1)}, bf16[48,1024]{1,0:T(8,128)(2,1)S(1)}, u32[]{:S(2)}, u32[]{:S(2)}) collective-permute-start(bf16[48,1024]{1,0:T(8,128)(2,1)S(1)} %shard_map.47), channel_id=1, source_target_pairs={{0,3},{1,2},{2,1},{3,0},{4,7},{5,6},{6,5},{7,4},{8,11},{9,10},{10,... | collective-permute-start | bytes 294920 | tf_op jit(solution)/shard_map/ppermute | solution.py:126
  13.4 5.7 %collective-permute-start.3 = (bf16[48,1024]{1,0:T(8,128)(2,1)S(1)}, bf16[48,1024]{1,0:T(8,128)(2,1)S(1)}, u32[]{:S(2)}, u32[]{:S(2)}) collective-permute-start(bf16[48,1024]{1,0:T(8,128)(2,1)S(1)} %shard_map.47), channel_id=1, source_target_pairs={{0,1},{1,0},{2,3},{3,2},{4,5},{5,4},{6,7},{7,6},{8,9},{9,8},{10,11... | collective-permute-start | bytes 294920 | tf_op jit(solution)/shard_map/ppermute | solution.py:126
  14.9 4.8 %collective-permute-start.2 = (bf16[48,1024]{1,0:T(8,128)(2,1)S(1)}, bf16[48,1024]{1,0:T(8,128)(2,1)S(1)}, u32[]{:S(2)}, u32[]{:S(2)}) collective-permute-start(bf16[48,1024]{1,0:T(8,128)(2,1)S(1)} %shard_map.47), channel_id=1, source_target_pairs={{0,2},{1,3},{2,0},{3,1},{4,6},{5,7},{6,4},{7,5},{8,10},{9,11},{10,... | collective-permute-start | bytes 294920 | tf_op jit(solution)/shard_map/ppermute | solution.py:126
  17.1 2.7 %collective-permute-start.7 = (bf16[1024,256]{1,0:T(8,128)(2,1)S(1)}, bf16[1024,256]{1,0:T(8,128)(2,1)S(1)}, u32[]{:S(2)}, u32[]{:S(2)}) collective-permute-start(bf16[1024,256]{1,0:T(8,128)(2,1)S(1)} %get-tuple-element.33.refs_4_.refs_0_), channel_id=1, source_target_pairs={{0,8},{8,0},{16,24},{24,16},{1,9},{9,1},{17,25},{25,17},{2,10},{10... | collective-permute-start | bytes 1572872 | tf_op jit(solution)/shard_map/ppermute | solution.py:126
  17.5 2.3 %collective-permute-start.8 = (bf16[1024,256]{1,0:T(8,128)(2,1)S(1)}, bf16[1024,256]{1,0:T(8,128)(2,1)S(1)}, u32[]{:S(2)}, u32[]{:S(2)}) collective-permute-start(bf16[1024,256]{1,0:T(8,128)(2,1)S(1)} %collective-permute-done.6.refs_5_.refs_1_), channel_id=1, source_target_pairs={{0,8},{8,0},{16,24},{24,16},{1,9},{9,1},{17,25},{25,17},{2,10},{10... | collective-permute-start | bytes 1572872 | tf_op jit(solution)/shard_map/ppermute | solution.py:126
